TPU v7x, 32 devices: a whole 2x2x4 slice. The times are simulated.
32 devices in a mesh: section: 2 (over x), batch: 4 (over z), tensor: 4 (over y, core).
Axes of the slice: x: 2, y: 2, z: 4, core: 2. Of those that a mesh axis runs over, the one named last changes fastest.
Arguments:
- patches: bfloat16 [2, 3200, 768], P(None, ('batch', 'tensor')), may hold values from -6 to 6
- cotangent: bfloat16 [2, 3200, 768], P(None, ('batch', 'tensor')), may hold values from -6 to 6
- image_lengths: int32 [2, 4, 60], P(None, 'batch'), may hold values from 0 to 800, as said below
- attn_gain: bfloat16 [2, 768], P('section'), may hold values from 0.5 to 1.5
- qkv_weight: bfloat16 [2, 768, 3, 768], P('section', None, None, 'tensor'), may hold values from -0.21875 to 0.21875
- query_gain: bfloat16 [2, 12, 64], P('section', 'tensor'), may hold values from 0.25 to 1.75
- key_gain: bfloat16 [2, 12, 64], P('section', 'tensor'), may hold values from 0.25 to 1.75
- out_weight: bfloat16 [2, 768, 768], P('section', 'tensor'), may hold values from -0.875 to 0.875
- mlp_gain: bfloat16 [2, 768], P('section'), may hold values from 0.5 to 1.5
- up_weight: bfloat16 [2, 768, 3072], P('section', None, 'tensor'), may hold values from -0.21875 to 0.21875
- down_weight: bfloat16 [2, 3072, 768], P('section', 'tensor'), may hold values from -0.109375 to 0.109375
Outputs:
- layer_outs: bfloat16 [2, 2, 3200, 768], P('section', None, ('batch', 'tensor'))
- input_grads: float32 [2, 2, 3200, 768], P('section', None, ('batch', 'tensor'))
- grad_attn_gain: float32 [2, 768], P('section')
- grad_qkv: float32 [2, 768, 3, 768], P('section', None, None, 'tensor')
- grad_query_gain: float32 [2, 12, 64], P('section', 'tensor')
- grad_key_gain: float32 [2, 12, 64], P('section', 'tensor')
- grad_out: float32 [2, 768, 768], P('section', 'tensor')
- grad_mlp_gain: float32 [2, 768], P('section')
- grad_up: float32 [2, 768, 3072], P('section', None, 'tensor')
- grad_down: float32 [2, 3072, 768], P('section', 'tensor')
Inputs may be any that keep to these rules, and one draw needn't show every extreme that they name: Row s of image_lengths lists the patch counts of the images of packed sequence s: 1 to 60 images, each of 1 patch or more, come first and the remaining entries are 0; a row sums to at most 800, and its slots past that sum are padding. The sizes are heavy-tailed.
All inputs are finite; a program needn't handle non-finite values.
Results may differ from a plain program's by a relative error of at most 0.035.
Values may be sent and summed in bfloat16 or wider, within the bound.
A program may use at most 192 MiB of HBM per device.

v0:
```python
import jax
import jax.numpy as jnp
from jax import lax
from jax.sharding import PartitionSpec as P

HEAD = 64
MICRO = 2


epsilon = 1e-06
neg_fill = -1000000000.0


def passed_along(block, axis, distance):
    devices = range(lax.axis_size(axis))
    route = [(i - distance, i) for i in devices if i - distance in devices]
    return lax.ppermute(block, axis, route)


def norm_rows(rows_in, gain_vec):
    centre = rows_in - jnp.mean(rows_in, axis=-1, keepdims=True)
    spread = jnp.mean(centre * centre, axis=-1, keepdims=True)
    return centre * lax.rsqrt(spread + epsilon) * gain_vec


def gelu_exact(rows_in):
    return jax.nn.gelu(rows_in, approximate=False)


def segment_ids(len_table, seq_len):
    bounds = jnp.cumsum(len_table, axis=-1, dtype=jnp.int32)
    places = jnp.arange(seq_len, dtype=jnp.int32)
    return jnp.sum((places[None, :, None] >= bounds[:, None, :]).astype(jnp.int32), axis=-1)


def select_where(flag_on, fresh_val, old_val):
    return jax.tree.map(lambda a, b: jnp.where(flag_on, a, b), fresh_val, old_val)


def attention_inputs(projected, len_table, query_gain, key_gain):
    seq_count = len_table.shape[0]
    seq_len = projected.shape[0] // seq_count
    head_count = projected.shape[2]
    grid_shape = (seq_count, seq_len, head_count, HEAD)
    queries = norm_rows(projected[:, 0], query_gain).astype(jnp.bfloat16).reshape(grid_shape)
    key_rows = norm_rows(projected[:, 1], key_gain).astype(jnp.bfloat16).reshape(grid_shape)
    value_rows = projected[:, 2].astype(jnp.bfloat16).reshape(grid_shape)
    segments = segment_ids(len_table, seq_len)
    same_seg = (segments[:, :, None] == segments[:, None, :])[:, None]
    scores = jnp.einsum("sqhd,skhd->shqk", queries, key_rows, preferred_element_type=jnp.float32)
    scores = jnp.where(same_seg, HEAD ** (-0.5) * scores, neg_fill)
    return (queries, key_rows, value_rows, scores)


def forward_layer(layer_in, len_table, weights):
    attn_gain, qkv_weight, query_gain, key_gain, out_weight, mlp_gain, up_weight, down_weight = (
        weights
    )
    model_width = layer_in.shape[1]
    head_cols = qkv_weight.shape[2]
    qkv_flat = qkv_weight.reshape(model_width, 3 * head_cols)
    rows_part = lax.all_gather(
        norm_rows(layer_in, attn_gain).astype(jnp.bfloat16), "tensor", axis=0, tiled=True
    )
    normed = rows_part
    projected = jnp.dot(rows_part, qkv_flat, preferred_element_type=jnp.float32)
    full_rows = normed.shape[0]
    projected = projected.reshape(full_rows, 3, head_cols // HEAD, HEAD)
    queries, key_rows, value_rows, scores = attention_inputs(
        projected, len_table, query_gain, key_gain
    )
    row_max = jnp.max(scores, axis=-1, keepdims=True)
    exp_scores = jnp.exp(scores - row_max)
    exp_total = jnp.sum(exp_scores, axis=-1, keepdims=True)
    log_total = row_max + jnp.log(exp_total)
    probs_low = (exp_scores / exp_total).astype(jnp.bfloat16)
    mixed_out = jnp.einsum(
        "shqk,skhd->sqhd", probs_low, value_rows, preferred_element_type=jnp.float32
    )
    mixed_out = mixed_out.reshape(full_rows, head_cols).astype(jnp.bfloat16)
    residual = layer_in + lax.psum_scatter(
        jnp.dot(mixed_out, out_weight, preferred_element_type=jnp.float32).astype(jnp.bfloat16),
        "tensor",
        scatter_dimension=0,
        tiled=True,
    ).astype(jnp.float32)
    rows_part = lax.all_gather(
        norm_rows(residual, mlp_gain).astype(jnp.bfloat16), "tensor", axis=0, tiled=True
    )
    upper = jnp.dot(rows_part, up_weight, preferred_element_type=jnp.float32)
    activated = gelu_exact(upper).astype(jnp.bfloat16)
    result = residual + lax.psum_scatter(
        jnp.dot(activated, down_weight, preferred_element_type=jnp.float32).astype(jnp.bfloat16),
        "tensor",
        scatter_dimension=0,
        tiled=True,
    ).astype(jnp.float32)
    return (
        result,
        (layer_in, normed, projected, log_total, mixed_out, residual, rows_part, upper, activated),
    )


def backward_layer(grad_out, cache, len_table, weights):
    attn_gain, qkv_weight, query_gain, key_gain, out_weight, mlp_gain, up_weight, down_weight = (
        weights
    )
    layer_in, normed, projected, log_total, mixed_out, residual, second, upper, activated = cache
    model_width = grad_out.shape[1]
    head_cols = qkv_weight.shape[2]
    head_count = head_cols // HEAD
    full_rows = normed.shape[0]
    qkv_flat = qkv_weight.reshape(model_width, 3 * head_cols)
    rows_part = lax.all_gather(grad_out.astype(jnp.bfloat16), "tensor", axis=0, tiled=True)
    grad_mlp = rows_part
    grad_act = jnp.einsum("rd,fd->rf", rows_part, down_weight, preferred_element_type=jnp.float32)
    grad_down = jnp.einsum("rf,rd->fd", activated, grad_mlp, preferred_element_type=jnp.float32)
    grad_upper = jax.vjp(gelu_exact, upper)[1](grad_act)[0].astype(jnp.bfloat16)
    grad_up = jnp.einsum("rd,rf->df", second, grad_upper, preferred_element_type=jnp.float32)
    grad_second = lax.psum_scatter(
        jnp.einsum("rf,df->rd", grad_upper, up_weight, preferred_element_type=jnp.float32).astype(
            jnp.bfloat16
        ),
        "tensor",
        scatter_dimension=0,
        tiled=True,
    ).astype(jnp.float32)
    grad_resid, grad_mlp_gain = jax.vjp(norm_rows, residual, mlp_gain)[1](grad_second)
    grad_resid = grad_out + grad_resid
    rows_part = lax.all_gather(grad_resid.astype(jnp.bfloat16), "tensor", axis=0, tiled=True)
    grad_mixed = jnp.einsum(
        "rd,cd->rc", rows_part, out_weight, preferred_element_type=jnp.float32
    ).astype(jnp.bfloat16)
    grad_out_weight = jnp.einsum(
        "rc,rd->cd", mixed_out, rows_part, preferred_element_type=jnp.float32
    )
    queries, key_rows, value_rows, scores = attention_inputs(
        projected, len_table, query_gain, key_gain
    )
    grad_mixed = grad_mixed.reshape(queries.shape)
    probs_full = jnp.exp(scores - log_total)
    grad_values = jnp.einsum(
        "shqk,sqhd->skhd",
        probs_full.astype(jnp.bfloat16),
        grad_mixed,
        preferred_element_type=jnp.float32,
    )
    grad_probs = jnp.einsum(
        "sqhd,skhd->shqk", grad_mixed, value_rows, preferred_element_type=jnp.float32
    )
    row_inner = jnp.sum(probs_full * grad_probs, axis=-1, keepdims=True)
    grad_scores = (probs_full * (grad_probs - row_inner)).astype(jnp.bfloat16)
    score_scale = HEAD ** (-0.5)
    grad_queries = (
        score_scale
        * jnp.einsum("shqk,skhd->sqhd", grad_scores, key_rows, preferred_element_type=jnp.float32)
    ).astype(jnp.bfloat16)
    grad_keys = (
        score_scale
        * jnp.einsum("shqk,sqhd->skhd", grad_scores, queries, preferred_element_type=jnp.float32)
    ).astype(jnp.bfloat16)
    grad_queries = (
        lax.optimization_barrier(grad_queries)
        .astype(jnp.float32)
        .reshape(full_rows, head_count, HEAD)
    )
    grad_keys = (
        lax.optimization_barrier(grad_keys).astype(jnp.float32).reshape(full_rows, head_count, HEAD)
    )
    grad_q_raw, grad_query_gain = jax.vjp(norm_rows, projected[:, 0], query_gain)[1](grad_queries)
    grad_k_raw, grad_key_gain = jax.vjp(norm_rows, projected[:, 1], key_gain)[1](grad_keys)
    grad_projected = jnp.stack(
        [grad_q_raw, grad_k_raw, grad_values.reshape(full_rows, head_count, HEAD)], axis=1
    )
    grad_projected = grad_projected.astype(jnp.bfloat16).reshape(full_rows, 3 * head_cols)
    grad_qkv = jnp.einsum(
        "rd,rc->dc", normed, grad_projected, preferred_element_type=jnp.float32
    ).reshape(model_width, 3, head_cols)
    grad_normed = lax.psum_scatter(
        jnp.einsum(
            "rc,dc->rd", grad_projected, qkv_flat, preferred_element_type=jnp.float32
        ).astype(jnp.bfloat16),
        "tensor",
        scatter_dimension=0,
        tiled=True,
    ).astype(jnp.float32)
    grad_in, grad_attn_gain = jax.vjp(norm_rows, layer_in, attn_gain)[1](grad_normed)
    return (
        grad_resid + grad_in,
        (
            grad_attn_gain,
            grad_qkv,
            grad_query_gain,
            grad_key_gain,
            grad_out_weight,
            grad_mlp_gain,
            grad_up,
            grad_down,
        ),
    )


def shards(
    patches,
    cotangent,
    image_lengths,
    attn_gain,
    qkv_weight,
    query_gain,
    key_gain,
    out_weight,
    mlp_gain,
    up_weight,
    down_weight,
):
    weights = (
        attn_gain[0],
        qkv_weight[0],
        query_gain[0],
        key_gain[0],
        out_weight[0],
        mlp_gain[0],
        up_weight[0],
        down_weight[0],
    )
    section_id = lax.axis_index("section")
    own_rows = patches.shape[1]
    model_width = patches.shape[2]
    received = jnp.zeros((own_rows, model_width), jnp.bfloat16)
    layer_rows = [jnp.zeros((own_rows, model_width), jnp.bfloat16) for mb_index in range(MICRO)]
    stored = [None for mb_index in range(MICRO)]
    for step_index in range(MICRO + 1):
        current = step_index - section_id
        len_table = lax.dynamic_index_in_dim(
            image_lengths, jnp.clip(current, 0, MICRO - 1), 0, keepdims=False
        )
        layer_in = jnp.where(section_id == 0, patches[min(step_index, MICRO - 1)], received).astype(
            jnp.float32
        )
        result, cache = forward_layer(layer_in, len_table, weights)
        sent_out = result.astype(jnp.bfloat16)
        if step_index < MICRO:
            received = passed_along(sent_out, "section", 1)
        kept_now = cache
        for mb_index in range(MICRO):
            if mb_index == step_index:
                stored[mb_index] = kept_now
            elif mb_index < step_index:
                stored[mb_index] = select_where(current == mb_index, kept_now, stored[mb_index])
            layer_rows[mb_index] = jnp.where(current == mb_index, sent_out, layer_rows[mb_index])
    incoming = jnp.zeros((own_rows, model_width), jnp.bfloat16)
    input_rows = [jnp.zeros((own_rows, model_width), jnp.float32) for mb_index in range(MICRO)]
    weight_totals = None
    gain_totals = None
    for step_index in range(MICRO + 1):
        current = step_index - 1 + section_id
        mb_slot = jnp.clip(current, 0, MICRO - 1)
        len_table = lax.dynamic_index_in_dim(image_lengths, mb_slot, 0, keepdims=False)
        grad_out = jnp.where(
            section_id == 1, cotangent[min(step_index, MICRO - 1)], incoming
        ).astype(jnp.float32)
        kept_now = stored[0]
        mb_index = 1
        kept_now = select_where(mb_slot == mb_index, stored[mb_index], kept_now)
        cache = kept_now
        grad_in, grad_set = backward_layer(grad_out, cache, len_table, weights)
        is_valid = (current >= 0) & (current < MICRO)
        grad_set = tuple((jnp.where(is_valid, g, 0.0) for g in grad_set))
        gain_one, qkv_grad, query_grad, key_grad, out_grad, gain_two, up_grad, down_grad = grad_set
        weight_now = (qkv_grad, query_grad, key_grad, out_grad, up_grad, down_grad)
        gain_now = (gain_one, gain_two)
        if weight_totals is None:
            weight_totals = weight_now
            gain_totals = gain_now
        else:
            weight_totals = tuple((a + b for a, b in zip(weight_totals, weight_now)))
            gain_totals = tuple((a + b for a, b in zip(gain_totals, gain_now)))
        rounded = grad_in.astype(jnp.bfloat16)
        if step_index < MICRO:
            incoming = passed_along(rounded, "section", -1)
        kept_grad = jnp.where(
            section_id == 1, lax.optimization_barrier(rounded).astype(jnp.float32), grad_in
        )
        for mb_index in range(MICRO):
            input_rows[mb_index] = jnp.where(current == mb_index, kept_grad, input_rows[mb_index])
    weight_totals = (
        lax.psum(weight_totals[0].astype(jnp.bfloat16), "batch").astype(jnp.float32),
        lax.psum(weight_totals[1], "batch").astype(jnp.float32),
        lax.psum(weight_totals[2], "batch").astype(jnp.float32),
        lax.psum(weight_totals[3].astype(jnp.bfloat16), "batch").astype(jnp.float32),
        lax.psum(weight_totals[4].astype(jnp.bfloat16), "batch").astype(jnp.float32),
        lax.psum(weight_totals[5].astype(jnp.bfloat16), "batch").astype(jnp.float32),
    )
    gain_one, gain_two = lax.psum(
        (gain_totals[0].astype(jnp.float32), gain_totals[1].astype(jnp.float32)),
        ("batch", "tensor"),
    )
    qkv_grad, query_grad, key_grad, out_grad, up_grad, down_grad = weight_totals
    return (
        jnp.stack(layer_rows)[None],
        jnp.stack(input_rows)[None],
        gain_one[None],
        qkv_grad[None],
        query_grad[None],
        key_grad[None],
        out_grad[None],
        gain_two[None],
        up_grad[None],
        down_grad[None],
    )


def solution(mesh):
    return jax.shard_map(
        shards,
        mesh=mesh,
        in_specs=(
            P(None, ("batch", "tensor"), None),
            P(None, ("batch", "tensor"), None),
            P(None, "batch", None),
            P("section", None),
            P("section", None, None, "tensor"),
            P("section", "tensor", None),
            P("section", "tensor", None),
            P("section", "tensor", None),
            P("section", None),
            P("section", None, "tensor"),
            P("section", "tensor", None),
        ),
        out_specs=(
            P("section", None, ("batch", "tensor"), None),
            P("section", None, ("batch", "tensor"), None),
            P("section", None),
            P("section", None, None, "tensor"),
            P("section", "tensor", None),
            P("section", "tensor", None),
            P("section", "tensor", None),
            P("section", None),
            P("section", None, "tensor"),
            P("section", "tensor", None),
        ),
        check_vma=False,
    )
```

profile of v0, /device:TPU:0, one launch (start us, length us, event | category | flops | bytes accessed | tf_op | source)
XLA Modules:
  0.0 953.8 jit_solution(4208172829879293233)
XLA Ops:
  15.4 17.4 %all-gather.14.cloned.1.call-done = bf16[800,768]{1,0:T(8,128)(2,1)} async-done(((bf16[200,768]{1,0:T(8,128)(2,1)}), bf16[800,768]{1,0:T(8,128)(2,1)}) %all-gather.14.cloned.1.call-update) | async-done | bytes 1228816 | tf_op jit(solution)/shard_map/all_gather | solution.py:62
  45.5 26.1 %reduce-scatter.13.cloned.1.call-done = bf16[200,768]{1,0:T(8,128)(2,1)} async-done(((bf16[800,768]{1,0:T(8,128)(2,1)}), bf16[200,768]{1,0:T(8,128)(2,1)}) %reduce-scatter.13.cloned.1.call-update) | async-done | bytes 307216 | tf_op jit(solution)/shard_map/reduce_scatter | solution.py:81
  76.2 17.6 %all-gather.16.cloned.1.call-done = bf16[800,768]{1,0:T(8,128)(2,1)} async-done(((bf16[200,768]{1,0:T(8,128)(2,1)}), bf16[800,768]{1,0:T(8,128)(2,1)}) %all-gather.16.cloned.1.call-update) | async-done | bytes 1228816 | tf_op jit(solution)/shard_map/all_gather | solution.py:87
  106.5 26.1 %reduce-scatter.15.cloned.1.call-done = bf16[200,768]{1,0:T(8,128)(2,1)} async-done(((bf16[800,768]{1,0:T(8,128)(2,1)}), bf16[200,768]{1,0:T(8,128)(2,1)}) %reduce-scatter.15.cloned.1.call-update) | async-done | bytes 307216 | tf_op jit(solution)/shard_map/reduce_scatter | solution.py:92
  146.0 17.8 %all-gather.18.cloned.1.call-done = bf16[800,768]{1,0:T(8,128)(2,1)} async-done(((bf16[200,768]{1,0:T(8,128)(2,1)}), bf16[800,768]{1,0:T(8,128)(2,1)}) %all-gather.18.cloned.1.call-update) | async-done | bytes 1228816 | tf_op jit(solution)/shard_map/all_gather | solution.py:62
  176.0 26.1 %reduce-scatter.17.cloned.1.call-done = bf16[200,768]{1,0:T(8,128)(2,1)} async-done(((bf16[800,768]{1,0:T(8,128)(2,1)}), bf16[200,768]{1,0:T(8,128)(2,1)}) %reduce-scatter.17.cloned.1.call-update) | async-done | bytes 307216 | tf_op jit(solution)/shard_map/reduce_scatter | solution.py:81
  206.4 10.3 %reduce-scatter.19.cloned.1.call-start = ((), (), s32[]{:S(2)}) async-start(), calls=%async_computation.19 | async-start | bytes 1536000 | tf_op jit(solution)/shard_map/reduce_scatter | solution.py:92
  235.6 26.1 %reduce-scatter.19.cloned.1.call-done = bf16[200,768]{1,0:T(8,128)(2,1)} async-done(((bf16[800,768]{1,0:T(8,128)(2,1)}), bf16[200,768]{1,0:T(8,128)(2,1)}) %reduce-scatter.19.cloned.1.call-update) | async-done | bytes 307216 | tf_op jit(solution)/shard_map/reduce_scatter | solution.py:92
  277.6 17.0 %all-gather.22.cloned.1.call-done = bf16[800,768]{1,0:T(8,128)(2,1)} async-done(((bf16[200,768]{1,0:T(8,128)(2,1)}), bf16[800,768]{1,0:T(8,128)(2,1)}) %all-gather.22.cloned.1.call-update) | async-done | bytes 1228816 | tf_op jit(solution)/shard_map/all_gather | solution.py:62
  311.7 25.5 %reduce-scatter.21.cloned.1.call-done = bf16[200,768]{1,0:T(8,128)(2,1)} async-done(((bf16[800,768]{1,0:T(8,128)(2,1)}), bf16[200,768]{1,0:T(8,128)(2,1)}) %reduce-scatter.21.cloned.1.call-update) | async-done | bytes 307216 | tf_op jit(solution)/shard_map/reduce_scatter | solution.py:81
  345.4 15.9 %all-gather.24.cloned.1.call-done = bf16[800,768]{1,0:T(8,128)(2,1)} async-done(((bf16[200,768]{1,0:T(8,128)(2,1)}), bf16[800,768]{1,0:T(8,128)(2,1)}) %all-gather.24.cloned.1.call-update) | async-done | bytes 1228816 | tf_op jit(solution)/shard_map/all_gather | solution.py:87
  361.3 9.1 select_select_fusion.2
  401.3 17.0 %reduce-scatter.25.cloned.1.call-done = bf16[200,768]{1,0:T(8,128)(2,1)} async-done(((bf16[800,768]{1,0:T(8,128)(2,1)}), bf16[200,768]{1,0:T(8,128)(2,1)}) %reduce-scatter.25.cloned.1.call-update) | async-done | bytes 307216 | tf_op jit(solution)/shard_map/reduce_scatter | solution.py:120
  465.0 26.1 %reduce-scatter.27.cloned.1.call-done = bf16[200,768]{1,0:T(8,128)(2,1)} async-done(((bf16[800,768]{1,0:T(8,128)(2,1)}), bf16[200,768]{1,0:T(8,128)(2,1)}) %reduce-scatter.27.cloned.1.call-update) | async-done | bytes 307216 | tf_op jit(solution)/shard_map/reduce_scatter | solution.py:179
  499.3 9.6 %collective-permute-done.2 = bf16[200,768]{1,0:T(8,128)(2,1)S(1)} collective-permute-done((bf16[200,768]{1,0:T(8,128)(2,1)S(1)}, bf16[200,768]{1,0:T(8,128)(2,1)S(1)}, u32[]{:S(2)}, u32[]{:S(2)}) %collective-permute-start.2) | collective-permute-done | bytes 307232 | tf_op jit(solution)/shard_map/ppermute | solution.py:17
  509.7 17.0 %all-gather.28.cloned.1.call-done = bf16[800,768]{1,0:T(8,128)(2,1)} async-done(((bf16[200,768]{1,0:T(8,128)(2,1)}), bf16[800,768]{1,0:T(8,128)(2,1)}) %all-gather.28.cloned.1.call-update) | async-done | bytes 1228816 | tf_op jit(solution)/shard_map/all_gather | solution.py:114
  546.0 19.3 %reduce-scatter.29.cloned.1.call-done = bf16[200,768]{1,0:T(8,128)(2,1)} async-done(((bf16[800,768]{1,0:T(8,128)(2,1)}), bf16[200,768]{1,0:T(8,128)(2,1)}) %reduce-scatter.29.cloned.1.call-update) | async-done | bytes 307216 | tf_op jit(solution)/shard_map/reduce_scatter | solution.py:120
  612.4 26.0 %reduce-scatter.31.cloned.1.call-done = bf16[200,768]{1,0:T(8,128)(2,1)} async-done(((bf16[800,768]{1,0:T(8,128)(2,1)}), bf16[200,768]{1,0:T(8,128)(2,1)}) %reduce-scatter.31.cloned.1.call-update) | async-done | bytes 307216 | tf_op jit(solution)/shard_map/reduce_scatter | solution.py:179
  645.9 9.6 %collective-permute-done.3 = bf16[200,768]{1,0:T(8,128)(2,1)S(1)} collective-permute-done((bf16[200,768]{1,0:T(8,128)(2,1)S(1)}, bf16[200,768]{1,0:T(8,128)(2,1)S(1)}, u32[]{:S(2)}, u32[]{:S(2)}) %collective-permute-start.3) | collective-permute-done | bytes 307232 | tf_op jit(solution)/shard_map/ppermute | solution.py:17
  656.3 16.9 %all-gather.32.cloned.1.call-done = bf16[800,768]{1,0:T(8,128)(2,1)} async-done(((bf16[200,768]{1,0:T(8,128)(2,1)}), bf16[800,768]{1,0:T(8,128)(2,1)}) %all-gather.32.cloned.1.call-update) | async-done | bytes 1228816 | tf_op jit(solution)/shard_map/all_gather | solution.py:114
  691.4 20.3 %reduce-scatter.33.cloned.1.call-done = bf16[200,768]{1,0:T(8,128)(2,1)} async-done(((bf16[800,768]{1,0:T(8,128)(2,1)}), bf16[200,768]{1,0:T(8,128)(2,1)}) %reduce-scatter.33.cloned.1.call-update) | async-done | bytes 307216 | tf_op jit(solution)/shard_map/reduce_scatter | solution.py:120
  795.0 11.8 %all-reduce.1 = (bf16[1,3,64]{2,1,0:T(4,128)(2,1)S(1)}, bf16[1,3,64]{2,0,1:T(2,128)(2,1)S(1)}) all-reduce(bf16[1,3,64]{2,1,0:T(4,128)(2,1)S(1)} %add_bitcast_fusion, bf16[1,3,64]{2,0,1:T(2,128)(2,1)S(1)} %broadcast_in_dim.389), channel_id=1, replica_groups=mesh['section'=2,'batch'=4,'tensor'=4] {'batch'}, use_global_device_ids=true, to_apply=%region_113.114 | all-reduce | flops 384 | bytes 1536 | tf_op jit(solution)/shard_map/psum | solution.py:288
  812.8 33.1 %all-reduce = (f32[1,768]{1,0:T(1,128)}, f32[1,768]{1,0:T(1,128)}) all-reduce(f32[1,768]{1,0:T(1,128)S(1)} %broadcast_in_dim.382, f32[1,768]{1,0:T(1,128)S(1)} %broadcast_in_dim.394), channel_id=1, replica_groups=mesh['section'=2,'batch'=4,'tensor'=4] {'batch','tensor'}, use_global_device_ids=true, to_apply=%region_108.109 | all-reduce | flops 1536 | bytes 12288 | tf_op jit(solution)/shard_map/psum | solution.py:294
  848.9 91.3 %all-reduce.5.cloned.1.call-done = (bf16[1,768,3,192]{1,3,2,0:T(8,128)(2,1)}, bf16[1,192,768]{2,1,0:T(8,128)(2,1)}, bf16[1,768,768]{2,1,0:T(8,128)(2,1)}, bf16[1,768,768]{2,1,0:T(8,128)(2,1)}) async-done(((bf16[1,768,3,192]{1,3,2,0:T(8,128)(2,1)}, bf16[1,192,768]{2,1,0:T(8,128)(2,1)}, bf16[1,768,768]{2,1,0:T(8,128)(2,1)}, bf16[1,768,768]{2,1,0:T(8,128)(2,1)}), (bf16[1,768,3,192]{1,3,2,0:T(8,128)(2,1)}, ...) | async-done | bytes 3538960 | tf_op jit(solution)/shard_map/psum | solution.py:287
  (685 shorter events, 403.9 us)
Async XLA Ops:
  12.2 59.4 %reduce-scatter.13.cloned.1.call-start = ((), (), s32[]{:S(2)}) async-start(), calls=%async_computation.13 | async-start | bytes 1536000 | tf_op jit(solution)/shard_map/reduce_scatter | solution.py:81
  45.4 48.3 %all-gather.16.cloned.1.call-start = ((), (), s32[]{:S(2)}) async-start(), calls=%async_computation.14 | async-start | bytes 1536000 | tf_op jit(solution)/shard_map/all_gather | solution.py:87
  75.9 56.7 %reduce-scatter.15.cloned.1.call-start = ((), (), s32[]{:S(2)}) async-start(), calls=%async_computation.15 | async-start | bytes 1536000 | tf_op jit(solution)/shard_map/reduce_scatter | solution.py:92
  106.4 57.5 %all-gather.18.cloned.1.call-start = ((), (), s32[]{:S(2)}) async-start(), calls=%async_computation.16 | async-start | bytes 1536000 | tf_op jit(solution)/shard_map/all_gather | solution.py:62
  145.0 57.2 %reduce-scatter.17.cloned.1.call-start = ((), (), s32[]{:S(2)}) async-start(), calls=%async_computation.17 | async-start | bytes 1536000 | tf_op jit(solution)/shard_map/reduce_scatter | solution.py:81
  176.0 48.3 %all-gather.20.cloned.1.call-start = ((), (), s32[]{:S(2)}) async-start(), calls=%async_computation.18 | async-start | bytes 1536000 | tf_op jit(solution)/shard_map/all_gather | solution.py:87
  206.4 55.4 %reduce-scatter.19.cloned.1.call-start = ((), (), s32[]{:S(2)}) async-start(), calls=%async_computation.19 | async-start | bytes 1536000 | tf_op jit(solution)/shard_map/reduce_scatter | solution.py:92
  235.6 59.0 %all-gather.22.cloned.1.call-start = ((), (), s32[]{:S(2)}) async-start(), calls=%async_computation.20 | async-start | bytes 1536000 | tf_op jit(solution)/shard_map/all_gather | solution.py:62
  275.7 61.5 %reduce-scatter.21.cloned.1.call-start = ((), (), s32[]{:S(2)}) async-start(), calls=%async_computation.21 | async-start | bytes 1536000 | tf_op jit(solution)/shard_map/reduce_scatter | solution.py:81
  311.6 49.6 %all-gather.24.cloned.1.call-start = ((), (), s32[]{:S(2)}) async-start(), calls=%async_computation.22 | async-start | bytes 1536000 | tf_op jit(solution)/shard_map/all_gather | solution.py:87
  343.3 37.2 %all-gather.36.cloned.1.call-start = ((), (), s32[]{:S(2)}) async-start(), calls=%async_computation.35 | async-start | bytes 1536000 | tf_op jit(solution)/shard_map/all_gather | solution.py:114
  345.1 73.1 %reduce-scatter.25.cloned.1.call-start = ((), (), s32[]{:S(2)}) async-start(), calls=%async_computation.24 | async-start | bytes 1536000 | tf_op jit(solution)/shard_map/reduce_scatter | solution.py:120
  392.0 49.4 %all-gather.26.cloned.1.call-start = ((), (), s32[]{:S(2)}) async-start(), calls=%async_computation.25 | async-start | bytes 1536000 | tf_op jit(solution)/shard_map/all_gather | solution.py:130
  423.5 67.6 %reduce-scatter.27.cloned.1.call-start = ((), (), s32[]{:S(2)}) async-start(), calls=%async_computation.26 | async-start | bytes 1536000 | tf_op jit(solution)/shard_map/reduce_scatter | solution.py:179
  464.9 61.8 %all-gather.28.cloned.1.call-start = ((), (), s32[]{:S(2)}) async-start(), calls=%async_computation.27 | async-start | bytes 1536000 | tf_op jit(solution)/shard_map/all_gather | solution.py:114
  509.7 55.5 %reduce-scatter.29.cloned.1.call-start = ((), (), s32[]{:S(2)}) async-start(), calls=%async_computation.28 | async-start | bytes 1536000 | tf_op jit(solution)/shard_map/reduce_scatter | solution.py:120
  539.0 50.1 %all-gather.30.cloned.1.call-start = ((), (), s32[]{:S(2)}) async-start(), calls=%async_computation.29 | async-start | bytes 1536000 | tf_op jit(solution)/shard_map/all_gather | solution.py:130
  571.2 67.3 %reduce-scatter.31.cloned.1.call-start = ((), (), s32[]{:S(2)}) async-start(), calls=%async_computation.30 | async-start | bytes 1536000 | tf_op jit(solution)/shard_map/reduce_scatter | solution.py:179
  612.4 60.9 %all-gather.32.cloned.1.call-start = ((), (), s32[]{:S(2)}) async-start(), calls=%async_computation.31 | async-start | bytes 1536000 | tf_op jit(solution)/shard_map/all_gather | solution.py:114
  656.3 55.5 %reduce-scatter.33.cloned.1.call-start = ((), (), s32[]{:S(2)}) async-start(), calls=%async_computation.32 | async-start | bytes 1536000 | tf_op jit(solution)/shard_map/reduce_scatter | solution.py:120
  685.5 66.5 %all-gather.34.cloned.1.call-start = ((), (), s32[]{:S(2)}) async-start(), calls=%async_computation.33 | async-start | bytes 1536000 | tf_op jit(solution)/shard_map/all_gather | solution.py:130
  717.7 74.6 %reduce-scatter.23.cloned.1.call-start = ((), (), s32[]{:S(2)}) async-start(), calls=%async_computation.23 | async-start | bytes 1536000 | tf_op jit(solution)/shard_map/reduce_scatter | solution.py:92
  733.0 74.9 %reduce-scatter.35.cloned.1.call-start = ((), (), s32[]{:S(2)}) async-start(), calls=%async_computation.34 | async-start | bytes 1536000 | tf_op jit(solution)/shard_map/reduce_scatter | solution.py:179
  775.2 165.0 %all-reduce.5.cloned.1.call-start = ((), (), s32[]{:S(2)}) async-start(), calls=%async_computation.36 | async-start | bytes 7077888 | tf_op jit(solution)/shard_map/psum | solution.py:287
  (191 other events, 2468.0 us)
Sparse Core Ops, SparseCore 0:
  12.3 20.4 all-gather.13
  45.6 26.0 reduce-scatter.12
  76.0 17.7 all-gather.15
  106.5 26.0 reduce-scatter.14
  145.1 18.7 all-gather.17
  176.1 26.0 reduce-scatter.16
  206.5 17.7 all-gather.19
  235.7 26.0 reduce-scatter.18
  275.8 18.7 all-gather.21
  311.7 25.3 reduce-scatter.20
  343.5 17.7 all-gather.23
  362.8 17.7 all-gather.35
  392.2 26.0 reduce-scatter.24
  423.6 17.7 all-gather.25
  465.0 26.0 reduce-scatter.26
  509.8 16.8 all-gather.27
  539.2 26.0 reduce-scatter.28
  571.3 17.7 all-gather.29
  612.5 25.9 reduce-scatter.30
  685.6 26.1 reduce-scatter.32
  717.8 17.7 all-gather.33
  738.2 26.0 reduce-scatter.22
  775.3 25.5 reduce-scatter.34
  804.7 135.4 all-reduce.4
  (1 shorter events, 16.8 us)
where the time goes:
time: 963 us; the launch traced here: 954 us
  waiting for transfers between devices  511 us (53%)
  matrix products  190 us (20%)
  other arithmetic  140 us (15%)
  blocking collectives  44.9 us (5%)
  local copies, waits for them, and re-layouts  28.9 us (3%)
  starting transfers between devices  22.2 us (2%)
  between operations  16.8 us (2%)
    psum x1, waiting for transfers between devices, shards(): lax.psum(weight_totals[0].astype(jnp.bfloat16), 'batch').astype(jnp.float32)  91.3 us
    reduce_scatter x3, waiting for transfers between devices, forward_layer(): lax.psum_scatter(jnp.dot(mixed_out, out_weight, preferred_element_type=jn...  77.7 us
    reduce_scatter x3, waiting for transfers between devices, backward_layer(): lax.psum_scatter(jnp.einsum('rf,df->rd', grad_upper, up_weight, preferred...  56.6 us
    reduce_scatter x3, waiting for transfers between devices, forward_layer(): lax.psum_scatter(jnp.dot(activated, down_weight, preferred_element_type=j...  52.3 us
    all_gather x3, waiting for transfers between devices, forward_layer(): lax.all_gather(norm_rows(layer_in, attn_gain).astype(jnp.bfloat16), 'tens...  52.2 us
    reduce_scatter x3, waiting for transfers between devices, backward_layer(): lax.psum_scatter(jnp.einsum('rc,dc->rd', grad_projected, qkv_flat, prefer...  52.2 us
    all_gather x3, waiting for transfers between devices, backward_layer(): lax.all_gather(grad_out.astype(jnp.bfloat16), 'tensor', axis=0, tiled=True)  41.4 us
    all_gather x3, waiting for transfers between devices, forward_layer(): lax.all_gather(norm_rows(residual, mlp_gain).astype(jnp.bfloat16), 'tenso...  41 us
  transfers between devices with their start and end apart: 29, of which 26 were waited for; matrix products, arithmetic and copies ran while one was open for 14% of the time, Pallas kernels for 0%

commit v1 on v0

v1 whole, which is shorter than its diff:
```python
import functools

import jax
import jax.numpy as jnp
from jax import lax
from jax.experimental import pallas as pl
from jax.experimental.pallas import tpu as pltpu
from jax.sharding import PartitionSpec as P

HEAD = 64
EPS = 1e-06
MESH = pl.DeviceIdType.MESH
BF = jnp.bfloat16
F32 = jnp.float32
KEY_BLOCK = 64
COLS = 256


def ceil_to(n, m):
    return -(-n // m) * m


def mm(a, b):
    return lax.dot_general(a, b, (((1,), (0,)), ((), ())), preferred_element_type=F32)


def mm_nt(a, b):
    return lax.dot_general(a, b, (((1,), (1,)), ((), ())), preferred_element_type=F32)


def mm_tn(a, b):
    return lax.dot_general(a, b, (((0,), (0,)), ((), ())), preferred_element_type=F32)


def normed(v):
    centre = v - jnp.mean(v, axis=-1, keepdims=True)
    r = lax.rsqrt(jnp.mean(centre * centre, axis=-1, keepdims=True) + EPS)
    return centre * r, r


def normed_back(dv, gain, xh, r):
    g = dv * gain
    return r * (g - jnp.mean(g, axis=-1, keepdims=True) - xh * jnp.mean(g * xh, axis=-1, keepdims=True))


def body(
    x_ref, ct_ref, segc_ref, segr_ref, sml_in, qkg_in, wq_in, wo_in, wu_in, wd_in,
    y_out, ig_out, gq_out, go_out, gu_out, gd_out, gg_out, gh_out,
    wq, wo, wu, wd, sml, qkg,
    xres, xh1, r1, xh2, r2,
    a_all, b_all, dm_all, da_all,
    qkh, qkr, qkvb, lse, o_t, g_all, gp_all,
    rows_buf, part, sendbuf, ysend, crecv, yrecv,
    e_buf, d_buf, dot_buf, dqkv_t,
    ybuf, dxbuf, ylo, dxlo,
    w_loc, w_send, w_recv, ag_s, ag_r, rs_s, rs_r, x_s, x_r,
):
    s, b, t = lax.axis_index("section"), lax.axis_index("batch"), lax.axis_index("tensor")
    y, c = t // 2, lax.rem(t, 2)
    core_id = (s, b, y * 2 + 1 - c)
    y_id = (s, b, (1 - y) * 2 + c)
    x_id = (1 - s, b, t)
    R, D = x_ref.shape
    N = 4 * R
    FF = wu.shape[2]
    HD = wo.shape[1]
    NH = HD // HEAD
    NB = N // KEY_BLOCK
    pos = c * 2 + y
    ypos = c * 2 + 1 - y
    own_rows = pl.ds(pl.multiple_of(pos * R, 16), R)
    y_rows = pl.ds(pl.multiple_of(ypos * R, 16), R)

    barrier = pltpu.get_barrier_semaphore()
    for peer in (core_id, y_id, x_id):
        pl.semaphore_signal(barrier, inc=1, device_id=peer, device_id_type=MESH)
    pl.semaphore_wait(barrier, 3)

    def remote(src, dst, ss, rs, peer):
        return pltpu.make_async_remote_copy(
            src_ref=src, dst_ref=dst, send_sem=ss, recv_sem=rs, device_id=peer, device_id_type=MESH
        )

    def arrived(ref, sem):
        pltpu.make_async_copy(ref, ref, sem).wait()

    moves = ((sml_in, sml), (qkg_in, qkg), (wq_in, wq), (wo_in, wo), (wu_in, wu), (wd_in, wd))
    for i, (src, dst) in enumerate(moves):
        remote(src, dst.at[s], w_send.at[i], w_recv.at[s, i], x_id).start()
        pltpu.make_async_copy(src, dst.at[s], w_loc.at[i]).start()
    for i, (src, dst) in enumerate(moves):
        pltpu.make_async_copy(src, dst.at[s], w_loc.at[i]).wait()

    def weights_here(l, i):
        @pl.when(l != s)
        def _():
            arrived(moves[i][1].at[1 - s], w_recv.at[1 - s, i])

    def gather_start(buf, l, op):
        mine = buf.at[l, own_rows]
        remote(mine, mine, ag_s.at[l, op, 0], ag_r.at[l, op, 0], core_id).start()
        remote(mine, mine, ag_s.at[l, op, 1], ag_r.at[l, op, 1], y_id).start()

    def gather_finish(buf, l, op):
        mine = buf.at[l, own_rows]
        theirs = buf.at[l, y_rows]
        arrived(theirs, ag_r.at[l, op, 1])
        third = remote(theirs, theirs, ag_s.at[l, op, 2], ag_r.at[l, op, 2], core_id)
        third.start()
        arrived(mine, ag_r.at[l, op, 0])
        arrived(mine, ag_r.at[l, op, 2])
        arrived(mine, ag_s.at[l, op, 0])
        arrived(mine, ag_s.at[l, op, 1])
        arrived(theirs, ag_s.at[l, op, 2])

    def scatter_start(product, l, op):
        slot = op % 2

        def send_tile(j, carry):
            cols = pl.ds(pl.multiple_of(j * COLS, COLS), COLS)
            sendbuf[:, cols] = product(pl.multiple_of((1 - c) * 2 * R, 16), cols).astype(BF)
            return carry

        lax.fori_loop(0, D // COLS, send_tile, 0)
        first = remote(sendbuf, crecv.at[slot], rs_s.at[l, op, 0], rs_r.at[l, op, 0], core_id)
        first.start()

        def own_tile(j, carry):
            cols = pl.ds(pl.multiple_of(j * COLS, COLS), COLS)
            part[:, cols] = product(pl.multiple_of(c * 2 * R, 16), cols)
            return carry

        lax.fori_loop(0, D // COLS, own_tile, 0)
        arrived(sendbuf, rs_r.at[l, op, 0])
        other = pl.ds(pl.multiple_of((1 - y) * R, 16), R)
        ysend[...] = (part[other] + crecv[slot, other].astype(F32)).astype(BF)
        remote(ysend, yrecv.at[slot], rs_s.at[l, op, 1], rs_r.at[l, op, 1], y_id).start()

    def scatter_finish(l, op):
        slot = op % 2
        mine = pl.ds(pl.multiple_of(y * R, 16), R)
        arrived(sendbuf, rs_s.at[l, op, 0])
        arrived(ysend, rs_s.at[l, op, 1])
        arrived(ysend, rs_r.at[l, op, 1])
        return part[mine] + crecv[slot, mine].astype(F32) + yrecv[slot].astype(F32)

    def q_rows(h):
        return pl.ds(pl.multiple_of(h * HEAD, HEAD), HEAD)

    def forward(l):
        weights_here(l, 0)
        weights_here(l, 1)
        xh, r = normed(xres[...])
        xh1[l] = xh
        r1[l] = r
        a_all[l, own_rows] = (xh * sml[l, 0:1]).astype(BF)
        gather_start(a_all, l, 0)
        weights_here(l, 2)
        gather_finish(a_all, l, 0)

        def project(i, carry):
            rows = pl.ds(pl.multiple_of(i * HD, HEAD), HD)
            qkvb[l, rows] = mm_nt(wq[l, rows], a_all[l]).astype(BF)
            return carry

        def project_normed(i, carry):
            rows = pl.ds(pl.multiple_of(i * HD, HEAD), HD)
            v = mm_nt(wq[l, rows], a_all[l])
            for h in range(NH):
                u = v[h * HEAD : (h + 1) * HEAD]
                u = u - jnp.mean(u, axis=0, keepdims=True)
                rr = lax.rsqrt(jnp.mean(u * u, axis=0, keepdims=True) + EPS)
                u = u * rr
                at = pl.ds(pl.multiple_of(i * HD + h * HEAD, HEAD), HEAD)
                qkh[l, at] = u
                qkr[l, i, pl.ds(h, 1)] = rr
                scale = jnp.where(i == 0, HEAD**-0.5, 1.0).astype(F32)
                gain = jnp.where(i == 0, qkg[l, :, h : h + 1], qkg[l, :, NH + h : NH + h + 1])
                qkvb[l, at] = ((u * gain).astype(BF).astype(F32) * scale).astype(BF)
            return carry

        lax.fori_loop(0, 2, project_normed, 0)
        project(2, 0)

        def head(h, carry):
            q_t = qkvb[l, q_rows(h)]
            k_rows = qkvb[l, q_rows(NH + h)].astype(F32).T.astype(BF)
            v_t = qkvb[l, q_rows(2 * NH + h)]
            rows_buf[0, :, :HEAD] = k_rows

            def block(i, total):
                at = pl.ds(pl.multiple_of(i * KEY_BLOCK, KEY_BLOCK), KEY_BLOCK)
                sc = mm(rows_buf[0, at, :HEAD], q_t)
                e = jnp.where(segc_ref[at] == segr_ref[...], jnp.exp(sc), 0.0)
                e_buf[at] = e.astype(BF)
                return total + jnp.sum(e, axis=0, keepdims=True)

            total = lax.fori_loop(0, NB, block, jnp.zeros((1, N), F32))
            lse[l, pl.ds(h, 1)] = jnp.log(total)
            o_t[l, q_rows(h)] = (mm(v_t, e_buf[...]) * (1.0 / total)).astype(BF)
            return carry

        lax.fori_loop(0, NH, head, 0)
        rows_buf[1, :, :HD] = o_t[l].astype(F32).T.astype(BF)
        weights_here(l, 3)
        scatter_start(lambda at, cols: mm(rows_buf[1, pl.ds(at, 2 * R), :HD], wo[l, :, cols]), l, 0)
        residual = xres[...] + scatter_finish(l, 0)
        xres[...] = residual
        xh, r = normed(residual)
        xh2[l] = xh
        r2[l] = r
        b_all[l, own_rows] = (xh * sml[l, 1:2]).astype(BF)
        gather_start(b_all, l, 1)
        weights_here(l, 4)
        gather_finish(b_all, l, 1)

        def hidden(i, carry):
            rows = pl.ds(pl.multiple_of(lax.rem(i, 4) * R, 16), R)
            cols = pl.ds(pl.multiple_of((i // 4) * COLS, COLS), COLS)
            u = mm(b_all[l, rows], wu[l, :, cols])
            cdf = 0.5 * (1.0 + lax.erf(u * 0.7071067811865476))
            pdf = jnp.exp(-0.5 * u * u) * 0.3989422804014327
            g_all[l, rows, cols] = (u * cdf).astype(BF)
            gp_all[l, rows, cols] = (cdf + u * pdf).astype(BF)
            return carry

        lax.fori_loop(0, 4 * (FF // COLS), hidden, 0)
        weights_here(l, 5)
        scatter_start(lambda at, cols: mm(g_all[l, pl.ds(at, 2 * R)], wd[l, :, cols]), l, 1)
        out = xres[...] + scatter_finish(l, 1)
        rounded = out.astype(BF)
        ybuf[l] = rounded
        xres[...] = rounded.astype(F32)

    xres[...] = x_ref[...].astype(F32)

    def forward_step(l, carry):
        forward(l)
        return carry

    lax.fori_loop(0, 2, forward_step, 0)
    y_move = remote(ybuf.at[1 - s], ylo, x_s.at[0], x_r.at[0], x_id)
    y_move.start()

    def backward(l):
        dm_all[l, own_rows] = xres[...].astype(BF)
        gather_start(dm_all, l, 2)
        gather_finish(dm_all, l, 2)

        def hidden(i, carry):
            rows = pl.ds(pl.multiple_of(lax.rem(i, 4) * R, 16), R)
            cols = pl.ds(pl.multiple_of((i // 4) * COLS, COLS), COLS)
            dg = mm_nt(dm_all[l, rows], wd[l, cols])
            gp_all[l, rows, cols] = (dg * gp_all[l, rows, cols].astype(F32)).astype(BF)
            return carry

        lax.fori_loop(0, 4 * (FF // COLS), hidden, 0)
        scatter_start(lambda at, cols: mm_nt(gp_all[l, pl.ds(at, 2 * R)], wu[l, cols]), l, 2)

        def hidden_grads(i, carry):
            cols = pl.ds(pl.multiple_of(i * COLS, COLS), COLS)
            gd_out[l, cols] = mm_tn(g_all[l, :, cols], dm_all[l]).astype(BF)
            gu_out[l, cols] = mm_tn(b_all[l, :, cols], gp_all[l]).astype(BF)
            return carry

        lax.fori_loop(0, FF // COLS, hidden_grads, 0)
        db = scatter_finish(l, 2)
        gg_out[l, 1:2] = jnp.sum(db * xh2[l], axis=0, keepdims=True)
        dh = xres[...] + normed_back(db, sml[l, 1:2], xh2[l], r2[l])
        xres[...] = dh
        da_all[l, own_rows] = dh.astype(BF)
        gather_start(da_all, l, 3)
        gather_finish(da_all, l, 3)
        dot_buf[...] = mm_nt(wo[l], da_all[l]).astype(BF)
        go_out[l] = mm(o_t[l], da_all[l]).astype(BF)

        def head(h, carry):
            q_t = qkvb[l, q_rows(h)]
            k_t = qkvb[l, q_rows(NH + h)]
            v_t = qkvb[l, q_rows(2 * NH + h)]
            rows_buf[0, :, :HEAD] = k_t.astype(F32).T.astype(BF)
            rows_buf[1, :, :HEAD] = v_t.astype(F32).T.astype(BF)
            do_t = dot_buf[q_rows(h)]
            delta = jnp.sum(do_t.astype(F32) * o_t[l, q_rows(h)].astype(F32), axis=0, keepdims=True)
            log_total = lse[l, pl.ds(h, 1)]

            def block(i, carry):
                at = pl.ds(pl.multiple_of(i * KEY_BLOCK, KEY_BLOCK), KEY_BLOCK)
                sc = mm(rows_buf[0, at, :HEAD], q_t)
                p = jnp.where(segc_ref[at] == segr_ref[...], jnp.exp(sc - log_total), 0.0)
                dp = mm(rows_buf[1, at, :HEAD], do_t)
                e_buf[at] = p.astype(BF)
                d_buf[at] = (p * (dp - delta)).astype(BF)
                return carry

            lax.fori_loop(0, NB, block, 0)
            dqkv_t[q_rows(2 * NH + h)] = mm_nt(do_t, e_buf[...]).astype(BF)
            dk = mm_nt(q_t, d_buf[...])
            dq = mm(k_t, d_buf[...]) * (HEAD**-0.5)
            for i, dv in ((0, dq), (1, dk)):
                at = q_rows(i * NH + h)
                dv = dv.astype(BF).astype(F32)
                uh = qkh[l, at]
                gh_out[l, i, h] = jnp.sum(dv * uh, axis=1, keepdims=True)
                gain = gains_of(l, i, h)
                g = dv * gain
                back = g - jnp.mean(g, axis=0, keepdims=True) - uh * jnp.mean(g * uh, axis=0, keepdims=True)
                dqkv_t[at] = (qkr[l, i, pl.ds(h, 1)] * back).astype(BF)
            return carry

        def gains_of(l, i, h):
            out = qkg[l, :, i * NH : i * NH + 1]
            for k in range(1, NH):
                out = jnp.where(h == k, qkg[l, :, i * NH + k : i * NH + k + 1], out)
            return out

        lax.fori_loop(0, NH, head, 0)
        rows_buf[0] = dqkv_t[...].astype(F32).T.astype(BF)
        scatter_start(lambda at, cols: mm(rows_buf[0, pl.ds(at, 2 * R)], wq[l, :, cols]), l, 3)
        gq_out[l] = mm(dqkv_t[...], a_all[l]).astype(BF)
        da = scatter_finish(l, 3)
        gg_out[l, 0:1] = jnp.sum(da * xh1[l], axis=0, keepdims=True)
        dx = xres[...] + normed_back(da, sml[l, 0:1], xh1[l], r1[l])
        rounded = dx.astype(BF)
        dxbuf[l] = rounded
        kept = jnp.where(l == 0, dx, rounded.astype(F32))
        xres[...] = rounded.astype(F32)

        @pl.when(l == s)
        def _():
            ig_out[s] = kept

    xres[...] = ct_ref[...].astype(F32)

    def backward_step(i, carry):
        backward(1 - i)
        return carry

    lax.fori_loop(0, 2, backward_step, 0)
    dx_move = remote(dxbuf.at[1 - s], dxlo, x_s.at[1], x_r.at[1], x_id)
    dx_move.start()
    y_move.wait()
    y_out[s] = ybuf[s]
    y_out[1 - s] = ylo[...]
    for i, (src, dst) in enumerate(moves):
        arrived(dst.at[s], w_send.at[i])
    dx_move.wait()
    ig_out[1 - s] = dxlo[...].astype(F32)


def fused(x, ct, segc, segr, small, qk_gain, wq, wo, wu, wd):
    R, D = x.shape
    N = 4 * R
    QD, HD, FF = wq.shape[0], wo.shape[0], wu.shape[1]
    NH = HD // HEAD
    vmem = pl.BlockSpec(memory_space=pltpu.VMEM)
    hbm = pl.BlockSpec(memory_space=pl.ANY)
    shape = jax.ShapeDtypeStruct
    V = pltpu.VMEM
    dma = pltpu.SemaphoreType.DMA
    return pl.pallas_call(
        body,
        out_shape=(
            shape((2, R, D), BF),
            shape((2, R, D), F32),
            shape((2, QD, D), BF),
            shape((2, HD, D), BF),
            shape((2, D, FF), BF),
            shape((2, FF, D), BF),
            shape((2, 8, D), F32),
            shape((2, 2, NH, HEAD, 1), F32),
        ),
        in_specs=[vmem] * 4 + [hbm] * 6,
        out_specs=(vmem,) * 8,
        scratch_shapes=[
            V((2, QD, D), BF), V((2, HD, D), BF), V((2, D, FF), BF), V((2, FF, D), BF),
            V((2, 8, D), F32), V((2, HEAD, 128), F32),
            V((R, D), F32), V((2, R, D), F32), V((2, R, 1), F32), V((2, R, D), F32), V((2, R, 1), F32),
            V((2, N, D), BF), V((2, N, D), BF), V((2, N, D), BF), V((2, N, D), BF),
            V((2, 2 * HD, N), F32), V((2, 2, 8, N), F32), V((2, QD, N), BF), V((2, 8, N), F32),
            V((2, HD, N), BF), V((2, N, FF), BF), V((2, N, FF), BF),
            V((2, N, QD), BF), V((2 * R, D), F32), V((2 * R, D), BF), V((R, D), BF),
            V((2, 2 * R, D), BF), V((2, R, D), BF),
            V((N, N), BF), V((N, N), BF), V((HD, N), BF), V((QD, N), BF),
            V((2, R, D), BF), V((2, R, D), BF), V((R, D), BF), V((R, D), BF),
            dma((6,)), dma((6,)), dma((2, 6)),
            dma((2, 4, 3)), dma((2, 4, 3)), dma((2, 4, 2)), dma((2, 4, 2)), dma((2,)), dma((2,)),
        ],
        name="layers",
        compiler_params=pltpu.CompilerParams(
            collective_id=0, has_side_effects=True, vmem_limit_bytes=63 * 2**20
        ),
    )(x, ct, segc, segr, small, qk_gain, wq, wo, wu, wd)


def shards(
    patches, cotangent, image_lengths, attn_gain, qkv_weight, query_gain, key_gain, out_weight,
    mlp_gain, up_weight, down_weight,
):
    s = lax.axis_index("section")
    _, own, D = patches.shape
    seq_len = 4 * own
    R = ceil_to(own, 16)
    N = 4 * R
    HD = out_weight.shape[1]
    NH = HD // HEAD
    pad = ((0, R - own), (0, 0))
    x = jnp.pad(lax.dynamic_index_in_dim(patches, s, 0, keepdims=False), pad)
    ct = jnp.pad(lax.dynamic_index_in_dim(cotangent, s, 0, keepdims=False), pad)
    lengths = lax.dynamic_index_in_dim(image_lengths, s, 0, keepdims=False)[0]
    bounds = jnp.cumsum(lengths, dtype=jnp.int32)
    places = jnp.arange(seq_len, dtype=jnp.int32)
    seg = jnp.sum((places[:, None] >= bounds[None, :]).astype(jnp.int32), axis=-1)
    seg = seg.reshape(2, 2, own).transpose(1, 0, 2).reshape(4, own)
    seg = jnp.pad(seg, ((0, 0), (0, R - own)), constant_values=-1).reshape(N)
    small = jnp.zeros((8, D), F32).at[0].set(attn_gain[0].astype(F32)).at[1].set(mlp_gain[0].astype(F32))
    qk_gain = jnp.concatenate([query_gain[0], key_gain[0]], axis=0).astype(F32).T
    qk_gain = jnp.pad(qk_gain, ((0, 0), (0, 128 - 2 * NH)))
    wq = qkv_weight[0].reshape(D, 3 * HD).T
    y, ig, gq, go, gu, gd, gg, gh = fused(
        x, ct, seg[:, None], seg[None, :], small, qk_gain, wq, out_weight[0], up_weight[0], down_weight[0]
    )

    def reduced(g):
        theirs = lax.ppermute(g[1 - s], "section", [(0, 1), (1, 0)])
        both = (g[s].astype(F32) + theirs.astype(F32)).astype(g.dtype)
        return both

    big = [reduced(g) for g in (gq, go, gu, gd)]
    gq, go, gu, gd = lax.psum(tuple(big), "batch")
    gg = lax.psum(gg[:, :2], ("section", "batch", "tensor"))[s]
    gh = lax.psum(gh[..., 0], ("section", "batch"))[s]
    return (
        y[:, :own][None],
        ig[:, :own][None],
        gg[0][None],
        gq.astype(F32).T.reshape(D, 3, HD)[None],
        gh[0][None],
        gh[1][None],
        go.astype(F32)[None],
        gg[1][None],
        gu.astype(F32)[None],
        gd.astype(F32)[None],
    )


def solution(mesh):
    return jax.shard_map(
        shards,
        mesh=mesh,
        in_specs=(
            P(None, ("batch", "tensor"), None),
            P(None, ("batch", "tensor"), None),
            P(None, "batch", None),
            P("section", None),
            P("section", None, None, "tensor"),
            P("section", "tensor", None),
            P("section", "tensor", None),
            P("section", "tensor", None),
            P("section", None),
            P("section", None, "tensor"),
            P("section", "tensor", None),
        ),
        out_specs=(
            P("section", None, ("batch", "tensor"), None),
            P("section", None, ("batch", "tensor"), None),
            P("section", None),
            P("section", None, None, "tensor"),
            P("section", "tensor", None),
            P("section", "tensor", None),
            P("section", "tensor", None),
            P("section", None),
            P("section", None, "tensor"),
            P("section", "tensor", None),
        ),
        check_vma=False,
    )
```

time: 963 us -> 539 us (0.56)
  waiting for transfers between devices: 511 us -> 140 us
  Pallas kernels: 0 us -> 290 us
  matrix products: 190 us -> 0 us
  other arithmetic: 140 us -> 12.1 us
  blocking collectives: 44.9 us -> 64.4 us
  starting transfers between devices: 22.2 us -> 4.12 us
  local copies, waits for them, and re-layouts: 28.9 us -> 13 us
    pallas_call x0 -> x1, Pallas kernels: none -> 290 us  [fused(): pl.pallas_call(body, out_shape=(shape((2, R, D), BF), shape((2, R, D), F3...]
    reduce_scatter x12 -> x0, waiting for transfers between devices: 239 us -> none  [the longest x3 77.7 us: forward_layer(): lax.psum_scatter(jnp.dot(mixed_out, out_weight, preferred_element_type=jn...]
    dot_general x57 -> x0, matrix products: 190 us -> none  [the longest x3 26.1 us: backward_layer(): jnp.einsum('rd,fd->rf', rows_part, down_weight, preferred_element_type=jn...]
    all_gather x12 -> x0, waiting for transfers between devices: 149 us -> none  [the longest x3 52.2 us: forward_layer(): lax.all_gather(norm_rows(layer_in, attn_gain).astype(jnp.bfloat16), 'tens...]
    reduce_sum x60 -> x1, other arithmetic: 59.3 us -> 0.11 us  [shards(): jnp.sum((places[:, None] >= bounds[None, :]).astype(jnp.int32), axis=-1)]
    ppermute x4, waiting for transfers between devices: 32.1 us -> 73 us  [reduced(): theirs = lax.ppermute(g[1 - s], 'section', [(0, 1), (1, 0)])]
    convert_element_type x21 -> x2, other arithmetic: 28.3 us -> 1.12 us  [the longest x1 1.12 us: reduced(): both = (g[s].astype(F32) + theirs.astype(F32)).astype(g.dtype)]
    unnamed x373 -> x32, local copies, waits for them, and re-layouts: 27.5 us -> 2.46 us
  transfers between devices with their start and end apart: 29 -> 5, of which waited for: 26 -> 2; matrix products, arithmetic and copies ran while one was open for 14% -> 1% of each run, Pallas kernels for 0% -> 0%
where the time goes in v1:
time: 539 us; the launch traced here: 538 us
  Pallas kernels  290 us (54%)
  waiting for transfers between devices  140 us (26%)
  blocking collectives  64.4 us (12%)
  between operations  14.2 us (3%)
  local copies, waits for them, and re-layouts  13 us (2%)
  other arithmetic  12.1 us (2%)
    pallas_call x1, Pallas kernels, fused(): pl.pallas_call(body, out_shape=(shape((2, R, D), BF), shape((2, R, D), F3...  290 us
    ppermute x4, waiting for transfers between devices, reduced(): theirs = lax.ppermute(g[1 - s], 'section', [(0, 1), (1, 0)])  73 us
    psum x1, waiting for transfers between devices, shards(): gq, go, gu, gd = lax.psum(tuple(big), 'batch')  67.3 us
    psum x1, blocking collectives, shards(): gg = lax.psum(gg[:, :2], ('section', 'batch', 'tensor'))[s]  42.5 us
    psum x1, blocking collectives, shards(): gh = lax.psum(gh[..., 0], ('section', 'batch'))[s]  21.9 us
  transfers between devices with their start and end apart: 5, of which 2 were waited for; matrix products, arithmetic and copies ran while one was open for 1% of the time, Pallas kernels for 0%

profile of v1, /device:TPU:0, one launch (start us, length us, event | category | flops | bytes accessed | tf_op | source)
XLA Modules:
  0.0 538.2 jit_solution(17187173470329522707)
XLA Ops:
  8.4 1.0 broadcast_in_dim_reshape.16.segc_ref
  10.1 1.1 dynamic-slice_bitcast_fusion.3
  11.2 0.7 pad.23.x_ref
  11.9 0.7 pad.24.ct_ref
  14.1 290.0 %layers.1 = (bf16[2,208,768]{2,1,0:T(8,128)(2,1)}, f32[2,208,768]{2,1,0:T(8,128)}, bf16[2,576,768]{2,1,0:T(8,128)(2,1)}, bf16[2,192,768]{2,1,0:T(8,128)(2,1)}, b...) custom-call(bf16[208,768]{1,0:T(8,128)(2,1)} %pad.23.x_ref, ...), custom_call_target="tpu_custom_call" | custom-call | tf_op jit(solution)/shard_map/layers/pallas_call | solution.py:361
  304.1 1.5 dynamic-slice_bitcast_fusion.1
  306.0 1.9 collective-permute-start
  308.3 1.9 collective-permute-start.1
  310.2 73.0 %collective-permute-done.1 = bf16[192,768]{1,0:T(8,128)(2,1)S(1)} collective-permute-done((bf16[192,768]{1,0:T(8,128)(2,1)S(1)}, bf16[192,768]{1,0:T(8,128)(2,1)S(1)}, u32[]{:S(2)}, u32[]{:S(2)}) %collective-permute-start.1) | collective-permute-done | bytes 294944 | tf_op jit(solution)/shard_map/ppermute | solution.py:425
  383.2 0.8 fusion.6
  384.0 1.1 fusion.2
  385.1 0.9 copy-done.2
  386.0 1.3 fusion.3
  387.3 1.3 fusion.4
  388.6 1.0 slice.64
  389.7 21.9 %psum.44 = f32[2,2,3,64]{3,1,2,0:T(2,128)S(1)} all-reduce(f32[2,2,3,64]{3,1,2,0:T(2,128)S(1)} %bitcast.64), channel_id=1, replica_groups=mesh['section'=2,'batch'=4,'tensor'=4] {'section','batch'}, use_global_device_ids=true, to_apply=%region_4.5 | all-reduce | flops 768 | bytes 6144 | tf_op jit(solution)/shard_map/psum | solution.py:432
  411.6 42.5 %psum.42 = f32[2,2,768]{2,1,0:T(2,128)S(1)} all-reduce(f32[2,2,768]{2,1,0:T(2,128)S(1)} %slice.64), channel_id=1, replica_groups=mesh['section'=2,'batch'=4,'tensor'=4] {'section','batch','tensor'}, use_global_device_ids=true, to_apply=%region_2.3 | all-reduce | flops 3072 | bytes 24576 | tf_op jit(solution)/shard_map/psum | solution.py:431
  455.3 0.9 slice_bitcast_fusion.1
  456.2 1.1 slice_bitcast_fusion
  457.3 67.3 %all-reduce.8.cloned.1.call-done = (bf16[1,768,3,192]{1,3,2,0:T(8,128)(2,1)}, bf16[1,192,768]{2,1,0:T(8,128)(2,1)}, bf16[1,768,768]{2,1,0:T(8,128)(2,1)}, bf16[1,768,768]{2,1,0:T(8,128)(2,1)}) async-done(((bf16[1,768,3,192]{1,3,2,0:T(8,128)(2,1)}, bf16[1,192,768]{2,1,0:T(8,128)(2,1)}, bf16[1,768,768]{2,1,0:T(8,128)(2,1)}, bf16[1,768,768]{2,1,0:T(8,128)(2,1)}), (bf16[1,768,3,192]{1,3,2,0:T(8,128)(2,1)}, ...) | async-done | bytes 3538960 | tf_op jit(solution)/shard_map/psum | solution.py:430
  524.6 2.6 broadcast_in_dim_reshape.15
  527.3 0.9 broadcast_in_dim.30
  528.1 1.6 broadcast_in_dim.32
  529.8 1.6 broadcast_in_dim.34
  (60 shorter events, 5.5 us)
Async XLA Ops:
  7.2 0.7 copy-start
  7.2 517.4 %all-reduce.8.cloned.1.call-start = ((), (), s32[]{:S(2)}) async-start(), calls=%async_computation | async-start | bytes 7077888 | tf_op jit(solution)/shard_map/psum | solution.py:430
  9.4 3.3 copy-start.12
  9.4 3.3 copy-start.13
  9.4 3.3 copy-start.14
  9.4 3.3 copy-start.15
  13.5 0.6 copy-start.11
  304.1 1.8 copy-start.3
  304.1 3.8 copy-start.1
  305.7 79.4 %collective-permute-start.2 = (bf16[768,768]{1,0:T(8,128)(2,1)S(1)}, bf16[768,768]{1,0:T(8,128)(2,1)S(1)}, u32[]{:S(2)}, u32[]{:S(2)}) collective-permute-start(bf16[768,768]{1,0:T(8,128)(2,1)S(1)} %dynamic-slice_bitcast_fusion.1), channel_id=1, source_target_pairs={{0,16},{16,0},{1,17},{17,1},{2,18},{18,2},{3,19},{19,3},{4,20},{20... | collective-permute-start | bytes 3538952 | tf_op jit(solution)/shard_map/ppermute | solution.py:425
  306.0 2.3 copy-start.8
  306.0 77.9 %collective-permute-start = (bf16[576,768]{1,0:T(8,128)(2,1)S(1)}, bf16[576,768]{1,0:T(8,128)(2,1)S(1)}, u32[]{:S(2)}, u32[]{:S(2)}) collective-permute-start(bf16[576,768]{1,0:T(8,128)(2,1)S(1)} %dynamic-slice_bitcast_fusion.2), channel_id=1, source_target_pairs={{0,16},{16,0},{1,17},{17,1},{2,18},{18,2},{3,19},{19,3},{4,20},{20... | collective-permute-start | bytes 2654216 | tf_op jit(solution)/shard_map/ppermute | solution.py:425
  308.0 79.3 %collective-permute-start.3 = (bf16[768,768]{1,0:T(8,128)(2,1)S(1)}, bf16[768,768]{1,0:T(8,128)(2,1)S(1)}, u32[]{:S(2)}, u32[]{:S(2)}) collective-permute-start(bf16[768,768]{1,0:T(8,128)(2,1)S(1)} %dynamic-slice_bitcast_fusion), channel_id=1, source_target_pairs={{0,16},{16,0},{1,17},{17,1},{2,18},{18,2},{3,19},{19,3},{4,20},{20... | collective-permute-start | bytes 3538952 | tf_op jit(solution)/shard_map/ppermute | solution.py:425
  308.3 74.9 %collective-permute-start.1 = (bf16[192,768]{1,0:T(8,128)(2,1)S(1)}, bf16[192,768]{1,0:T(8,128)(2,1)S(1)}, u32[]{:S(2)}, u32[]{:S(2)}) collective-permute-start(bf16[192,768]{1,0:T(8,128)(2,1)S(1)} %dynamic-slice_bitcast_fusion.5), channel_id=1, source_target_pairs={{0,16},{16,0},{1,17},{17,1},{2,18},{18,2},{3,19},{19,3},{4,20},{20... | collective-permute-start | bytes 884744 | tf_op jit(solution)/shard_map/ppermute | solution.py:425
  384.0 2.0 copy-start.2
  388.6 1.0 copy-start.9
  388.6 66.7 %copy-start.7 = (bf16[2,208,768]{2,1,0:T(8,128)(2,1)S(1)}, bf16[2,208,768]{2,1,0:T(8,128)(2,1)}, u32[]{:S(2)}) copy-start(bf16[2,208,768]{2,1,0:T(8,128)(2,1)} %get-tuple-element.42) | copy-start | bytes 1916932
  388.6 67.6 %copy-start.4 = (f32[2,208,768]{2,1,0:T(8,128)S(1)}, f32[2,208,768]{2,1,0:T(8,128)}, u32[]{:S(2)}) copy-start(f32[2,208,768]{2,1,0:T(8,128)} %get-tuple-element.43) | copy-start | bytes 3833860
  524.6 2.6 copy-start.10
  524.6 3.5 copy-start.6
  528.1 1.7 copy-start.5
Sparse Core Ops, SparseCore 0:
  388.7 135.8 all-reduce.7

commit v2 on v1

--- a/solution.py
+++ b/solution.py
@@ -14,6 +14,9 @@
 F32 = jnp.float32
 KEY_BLOCK = 64
 COLS = 256
+SUB = 192
+TAKEN = ((0, 0, 0, 1, 2, 3, 5, 7, 9, 10, 11, 12), (2, 3, 4, 6, 7, 9, 10, 11, 12, 12, 12, 12))
+LAYER_POINTS = 7
 
 
 def ceil_to(n, m):
@@ -44,8 +47,9 @@
 
 
 def body(
+    chain,
     x_ref, ct_ref, segc_ref, segr_ref, sml_in, qkg_in, wq_in, wo_in, wu_in, wd_in,
-    y_out, ig_out, gq_out, go_out, gu_out, gd_out, gg_out, gh_out,
+    y_out, ig_out, g_out, gg_out, gh_out,
     wq, wo, wu, wd, sml, qkg,
     xres, xh1, r1, xh2, r2,
     a_all, b_all, dm_all, da_all,
@@ -53,7 +57,10 @@
     rows_buf, part, sendbuf, ysend, crecv, yrecv,
     e_buf, d_buf, dot_buf, dqkv_t,
     ybuf, dxbuf, ylo, dxlo,
+    grads, gains, hgains,
     w_loc, w_send, w_recv, ag_s, ag_r, rs_s, rs_r, x_s, x_r,
+    gx, gz, gpart, gfin, gains_x, hgains_x, gains_z, hgains_z, gains_t,
+    gx_s, gx_r, gz_s, gz_r, g_loc, sm_s, sm_r,
 ):
     s, b, t = lax.axis_index("section"), lax.axis_index("batch"), lax.axis_index("tensor")
     y, c = t // 2, lax.rem(t, 2)
@@ -71,10 +78,12 @@
     own_rows = pl.ds(pl.multiple_of(pos * R, 16), R)
     y_rows = pl.ds(pl.multiple_of(ypos * R, 16), R)
 
+    diag_id = (s, b, (1 - y) * 2 + 1 - c)
+    z_ids = [(s, lax.rem(b + k, 4), t) for k in (1, 2, 3)] if chain else []
     barrier = pltpu.get_barrier_semaphore()
-    for peer in (core_id, y_id, x_id):
+    for peer in [core_id, y_id, diag_id, x_id] + z_ids:
         pl.semaphore_signal(barrier, inc=1, device_id=peer, device_id_type=MESH)
-    pl.semaphore_wait(barrier, 3)
+    pl.semaphore_wait(barrier, 4 + len(z_ids))
 
     def remote(src, dst, ss, rs, peer):
         return pltpu.make_async_remote_copy(
@@ -97,13 +106,15 @@
             arrived(moves[i][1].at[1 - s], w_recv.at[1 - s, i])
 
     def gather_start(buf, l, op):
-        mine = buf.at[l, own_rows]
+        part_of = l if op < 2 else 0
+        mine = buf.at[part_of, own_rows]
         remote(mine, mine, ag_s.at[l, op, 0], ag_r.at[l, op, 0], core_id).start()
         remote(mine, mine, ag_s.at[l, op, 1], ag_r.at[l, op, 1], y_id).start()
 
     def gather_finish(buf, l, op):
-        mine = buf.at[l, own_rows]
-        theirs = buf.at[l, y_rows]
+        part_of = l if op < 2 else 0
+        mine = buf.at[part_of, own_rows]
+        theirs = buf.at[part_of, y_rows]
         arrived(theirs, ag_r.at[l, op, 1])
         third = remote(theirs, theirs, ag_s.at[l, op, 2], ag_r.at[l, op, 2], core_id)
         third.start()
@@ -143,6 +154,130 @@
         arrived(ysend, rs_s.at[l, op, 1])
         arrived(ysend, rs_r.at[l, op, 1])
         return part[mine] + crecv[slot, mine].astype(F32) + yrecv[slot].astype(F32)
+
+    FD, UP, OUT = 0, FF, FF + D
+    QKV = OUT + HD
+    KS = grads.shape[1] // SUB
+    HALF = SUB // 2
+    middle = (b == 1) | (b == 2)
+    end = jnp.logical_not(middle)
+    inner_id = (s, jnp.where(b == 0, 1, 2), t)
+    outer_id = (s, jnp.where(b == 1, 0, 3), t)
+    partner_id = (s, jnp.where(b == 1, 2, 1), t)
+    mine_at = jnp.where(b == 1, 0, HALF)
+    other_at = HALF - mine_at
+
+    def sub_rows(k):
+        return pl.ds(pl.multiple_of(k * SUB, 16), SUB)
+
+    def half_rows(k, at):
+        return pl.ds(pl.multiple_of(k * SUB + at, 16), HALF)
+
+    def send_grads(l, lo, hi):
+        if not chain:
+            return
+
+        @pl.when(l != s)
+        def _():
+            def one(k, carry):
+                rows = sub_rows(k)
+                remote(grads.at[l, rows], gx.at[rows], gx_s.at[k], gx_r.at[k], x_id).start()
+                return carry
+
+            lax.fori_loop(lo, hi, one, 0)
+
+    def step1(k, carry):
+        rows = sub_rows(k)
+        arrived(gx.at[rows], gx_r.at[k])
+        grads[s, rows] = (grads[s, rows].astype(F32) + gx[rows].astype(F32)).astype(BF)
+
+        @pl.when(end)
+        def _():
+            remote(grads.at[s, rows], gz.at[rows], gz_s.at[0, k], gz_r.at[0, k], inner_id).start()
+
+        return carry
+
+    def step2(k, carry):
+        @pl.when(middle)
+        def _():
+            rows = sub_rows(k)
+            arrived(gz.at[rows], gz_r.at[0, k])
+            grads[s, rows] = (grads[s, rows].astype(F32) + gz[rows].astype(F32)).astype(BF)
+            other = grads.at[s, half_rows(k, other_at)]
+            remote(other, gpart.at[k], gz_s.at[0, k], gz_r.at[1, k], partner_id).start()
+
+        return carry
+
+    def step3(k, carry):
+        @pl.when(middle)
+        def _():
+            rows = half_rows(k, mine_at)
+            arrived(gpart.at[k], gz_r.at[1, k])
+            grads[s, rows] = (grads[s, rows].astype(F32) + gpart[k].astype(F32)).astype(BF)
+            done = grads.at[s, rows]
+            remote(done, gfin.at[k], gz_s.at[1, k], gz_r.at[2, k], partner_id).start()
+            remote(done, gz.at[rows], gz_s.at[2, k], gz_r.at[0, k], outer_id).start()
+            pltpu.make_async_copy(done, g_out.at[rows], g_loc.at[0, k]).start()
+
+        return carry
+
+    def step4(k, carry):
+        @pl.when(middle)
+        def _():
+            rows = half_rows(k, other_at)
+            arrived(gfin.at[k], gz_r.at[2, k])
+            remote(gfin.at[k], gz.at[rows], gz_s.at[3, k], gz_r.at[1, k], outer_id).start()
+            pltpu.make_async_copy(gfin.at[k], g_out.at[rows], g_loc.at[1, k]).start()
+
+        return carry
+
+    def step5(k, carry):
+        @pl.when(end)
+        def _():
+            rows = sub_rows(k)
+            arrived(gz.at[half_rows(k, 0)], gz_r.at[0, k])
+            arrived(gz.at[half_rows(k, HALF)], gz_r.at[1, k])
+            pltpu.make_async_copy(gz.at[rows], g_out.at[rows], g_loc.at[0, k]).start()
+
+        return carry
+
+    steps = (step1, step2, step3, step4, step5)
+    last_point = len(TAKEN[0]) + len(steps) - 1
+
+    def progress(point, live):
+        if not chain:
+            return
+
+        def taken(p):
+            if p < 0:
+                return 0
+            p = min(p, len(TAKEN[0]) - 1)
+            return jnp.where(live, jnp.where(s == 0, TAKEN[0][p], TAKEN[1][p]), 0)
+
+        for i, step in enumerate(steps):
+            lax.fori_loop(taken(point - i - 1), taken(point - i), step, 0)
+
+    def finish_grads():
+        def one(k, carry):
+            rows = sub_rows(k)
+            half = grads.at[1 - s, half_rows(k, 0)]
+            arrived(grads.at[1 - s, rows], gx_s.at[k])
+
+            @pl.when(end)
+            def _():
+                arrived(grads.at[s, rows], gz_s.at[0, k])
+                arrived(g_out.at[rows], g_loc.at[0, k])
+
+            @pl.when(middle)
+            def _():
+                for j in range(4):
+                    arrived(half, gz_s.at[j, k])
+                for j in range(2):
+                    arrived(g_out.at[half_rows(k, 0)], g_loc.at[j, k])
+
+            return carry
+
+        lax.fori_loop(0, KS, one, 0)
 
     def q_rows(h):
         return pl.ds(pl.multiple_of(h * HEAD, HEAD), HEAD)
@@ -243,36 +378,48 @@
     y_move.start()
 
     def backward(l):
-        dm_all[l, own_rows] = xres[...].astype(BF)
+        live = l == 0
+        dm_all[0, own_rows] = xres[...].astype(BF)
         gather_start(dm_all, l, 2)
+        progress(0, live)
         gather_finish(dm_all, l, 2)
 
         def hidden(i, carry):
             rows = pl.ds(pl.multiple_of(lax.rem(i, 4) * R, 16), R)
             cols = pl.ds(pl.multiple_of((i // 4) * COLS, COLS), COLS)
-            dg = mm_nt(dm_all[l, rows], wd[l, cols])
+            dg = mm_nt(dm_all[0, rows], wd[l, cols])
             gp_all[l, rows, cols] = (dg * gp_all[l, rows, cols].astype(F32)).astype(BF)
             return carry
 
         lax.fori_loop(0, 4 * (FF // COLS), hidden, 0)
+        progress(1, live)
         scatter_start(lambda at, cols: mm_nt(gp_all[l, pl.ds(at, 2 * R)], wu[l, cols]), l, 2)
 
         def hidden_grads(i, carry):
             cols = pl.ds(pl.multiple_of(i * COLS, COLS), COLS)
-            gd_out[l, cols] = mm_tn(g_all[l, :, cols], dm_all[l]).astype(BF)
-            gu_out[l, cols] = mm_tn(b_all[l, :, cols], gp_all[l]).astype(BF)
+            grads[l, pl.ds(pl.multiple_of(FD + i * COLS, COLS), COLS)] = mm_tn(
+                g_all[l, :, cols], dm_all[0]
+            ).astype(BF)
+            grads[l, pl.ds(pl.multiple_of(UP + i * COLS, COLS), COLS)] = mm_tn(
+                b_all[l, :, cols], gp_all[l]
+            ).astype(BF)
             return carry
 
         lax.fori_loop(0, FF // COLS, hidden_grads, 0)
+        send_grads(l, 0, OUT // SUB)
+        progress(2, live)
         db = scatter_finish(l, 2)
-        gg_out[l, 1:2] = jnp.sum(db * xh2[l], axis=0, keepdims=True)
+        gains[l, 1:2] = jnp.sum(db * xh2[l], axis=0, keepdims=True)
         dh = xres[...] + normed_back(db, sml[l, 1:2], xh2[l], r2[l])
         xres[...] = dh
-        da_all[l, own_rows] = dh.astype(BF)
+        da_all[0, own_rows] = dh.astype(BF)
         gather_start(da_all, l, 3)
+        progress(3, live)
         gather_finish(da_all, l, 3)
-        dot_buf[...] = mm_nt(wo[l], da_all[l]).astype(BF)
-        go_out[l] = mm(o_t[l], da_all[l]).astype(BF)
+        dot_buf[...] = mm_nt(wo[l], da_all[0]).astype(BF)
+        grads[l, OUT:QKV] = mm(o_t[l], da_all[0]).astype(BF)
+        send_grads(l, OUT // SUB, QKV // SUB)
+        progress(4, live)
 
         def head(h, carry):
             q_t = qkvb[l, q_rows(h)]
@@ -301,7 +448,8 @@
                 at = q_rows(i * NH + h)
                 dv = dv.astype(BF).astype(F32)
                 uh = qkh[l, at]
-                gh_out[l, i, h] = jnp.sum(dv * uh, axis=1, keepdims=True)
+                lanes = lax.broadcasted_iota(jnp.int32, (HEAD, 128), 1) == i * NH + h
+                hgains[l] = jnp.where(lanes, jnp.sum(dv * uh, axis=1, keepdims=True), hgains[l])
                 gain = gains_of(l, i, h)
                 g = dv * gain
                 back = g - jnp.mean(g, axis=0, keepdims=True) - uh * jnp.mean(g * uh, axis=0, keepdims=True)
@@ -314,12 +462,17 @@
                 out = jnp.where(h == k, qkg[l, :, i * NH + k : i * NH + k + 1], out)
             return out
 
+        hgains[l] = jnp.zeros((HEAD, 128), F32)
+        gains[l] = jnp.where(lax.broadcasted_iota(jnp.int32, (8, D), 0) == 1, gains[l], 0.0)
         lax.fori_loop(0, NH, head, 0)
+        progress(5, live)
         rows_buf[0] = dqkv_t[...].astype(F32).T.astype(BF)
         scatter_start(lambda at, cols: mm(rows_buf[0, pl.ds(at, 2 * R)], wq[l, :, cols]), l, 3)
-        gq_out[l] = mm(dqkv_t[...], a_all[l]).astype(BF)
+        grads[l, QKV:] = mm(dqkv_t[...], a_all[l]).astype(BF)
+        send_grads(l, QKV // SUB, KS)
+        progress(6, live)
         da = scatter_finish(l, 3)
-        gg_out[l, 0:1] = jnp.sum(da * xh1[l], axis=0, keepdims=True)
+        gains[l, 0:1] = jnp.sum(da * xh1[l], axis=0, keepdims=True)
         dx = xres[...] + normed_back(da, sml[l, 0:1], xh1[l], r1[l])
         rounded = dx.astype(BF)
         dxbuf[l] = rounded
@@ -330,6 +483,13 @@
         def _():
             ig_out[s] = kept
 
+        @pl.when(l != s)
+        def _():
+            remote(dxbuf.at[1 - s], dxlo, x_s.at[1], x_r.at[1], x_id).start()
+            if chain:
+                remote(gains.at[1 - s], gains_x, sm_s.at[0], sm_r.at[0], x_id).start()
+                remote(hgains.at[1 - s], hgains_x, sm_s.at[1], sm_r.at[1], x_id).start()
+
     xres[...] = ct_ref[...].astype(F32)
 
     def backward_step(i, carry):
@@ -337,18 +497,52 @@
         return carry
 
     lax.fori_loop(0, 2, backward_step, 0)
-    dx_move = remote(dxbuf.at[1 - s], dxlo, x_s.at[1], x_r.at[1], x_id)
-    dx_move.start()
+    progress(LAYER_POINTS, True)
+    if chain:
+        arrived(gains_x, sm_r.at[0])
+        arrived(hgains_x, sm_r.at[1])
+        gains_z[b] = gains[s] + gains_x[...]
+        hgains_z[b] = hgains[s] + hgains_x[...]
+        for i, peer in enumerate(z_ids):
+            remote(gains_z.at[b], gains_z.at[b], sm_s.at[2 + i], sm_r.at[2 + i], peer).start()
+            remote(hgains_z.at[b], hgains_z.at[b], sm_s.at[5 + i], sm_r.at[5 + i], peer).start()
+        progress(LAYER_POINTS + 1, True)
+        for i in range(3):
+            arrived(gains_x, sm_r.at[2 + i])
+            arrived(hgains_x, sm_r.at[5 + i])
+        gh_out[...] = hgains_z[0] + hgains_z[1] + hgains_z[2] + hgains_z[3]
+        gains_t[t] = gains_z[0] + gains_z[1] + gains_z[2] + gains_z[3]
+        for i, peer in enumerate((core_id, y_id, diag_id)):
+            remote(gains_t.at[t], gains_t.at[t], sm_s.at[8 + i], sm_r.at[8 + i], peer).start()
+        progress(LAYER_POINTS + 2, True)
+        for i in range(3):
+            arrived(gains_x, sm_r.at[8 + i])
+        gg_out[...] = gains_t[0] + gains_t[1] + gains_t[2] + gains_t[3]
+        for point in range(LAYER_POINTS + 3, last_point):
+            progress(point, True)
+    else:
+        g_out[...] = grads[...]
+        gg_out[...] = gains[...]
+        gh_out[...] = hgains[...]
     y_move.wait()
     y_out[s] = ybuf[s]
     y_out[1 - s] = ylo[...]
     for i, (src, dst) in enumerate(moves):
         arrived(dst.at[s], w_send.at[i])
-    dx_move.wait()
+    arrived(dxlo, x_s.at[1])
+    arrived(dxlo, x_r.at[1])
     ig_out[1 - s] = dxlo[...].astype(F32)
-
-
-def fused(x, ct, segc, segr, small, qk_gain, wq, wo, wu, wd):
+    if chain:
+        finish_grads()
+        for i in range(2, 5):
+            arrived(gains_x, sm_s.at[i])
+            arrived(hgains_x, sm_s.at[3 + i])
+            arrived(gains_x, sm_s.at[6 + i])
+        arrived(gains_x, sm_s.at[0])
+        arrived(hgains_x, sm_s.at[1])
+
+
+def fused(chain, x, ct, segc, segr, small, qk_gain, wq, wo, wu, wd):
     R, D = x.shape
     N = 4 * R
     QD, HD, FF = wq.shape[0], wo.shape[0], wu.shape[1]
@@ -358,34 +552,42 @@
     shape = jax.ShapeDtypeStruct
     V = pltpu.VMEM
     dma = pltpu.SemaphoreType.DMA
+    G = FF + D + HD + QD
+    KS = G // SUB
+    ahead = () if chain else (2,)
+    extra = [
+        V((G, D), BF), V((G, D), BF), V((KS, SUB // 2, D), BF), V((KS, SUB // 2, D), BF),
+        V((8, D), F32), V((HEAD, 128), F32), V((4, 8, D), F32), V((4, HEAD, 128), F32), V((4, 8, D), F32),
+        dma((KS,)), dma((KS,)), dma((4, KS)), dma((3, KS)), dma((2, KS)), dma((11,)), dma((11,)),
+    ]
+    if not chain:
+        extra = [V((8, 128), F32)] * 9 + [dma((1,))] * 7
     return pl.pallas_call(
-        body,
+        functools.partial(body, chain),
         out_shape=(
             shape((2, R, D), BF),
             shape((2, R, D), F32),
-            shape((2, QD, D), BF),
-            shape((2, HD, D), BF),
-            shape((2, D, FF), BF),
-            shape((2, FF, D), BF),
-            shape((2, 8, D), F32),
-            shape((2, 2, NH, HEAD, 1), F32),
+            shape(ahead + (G, D), BF),
+            shape(ahead + (8, D), F32),
+            shape(ahead + (HEAD, 128), F32),
         ),
         in_specs=[vmem] * 4 + [hbm] * 6,
-        out_specs=(vmem,) * 8,
+        out_specs=(vmem, vmem, hbm if chain else vmem, vmem, vmem),
         scratch_shapes=[
             V((2, QD, D), BF), V((2, HD, D), BF), V((2, D, FF), BF), V((2, FF, D), BF),
             V((2, 8, D), F32), V((2, HEAD, 128), F32),
             V((R, D), F32), V((2, R, D), F32), V((2, R, 1), F32), V((2, R, D), F32), V((2, R, 1), F32),
-            V((2, N, D), BF), V((2, N, D), BF), V((2, N, D), BF), V((2, N, D), BF),
+            V((2, N, D), BF), V((2, N, D), BF), V((1, N, D), BF), V((1, N, D), BF),
             V((2, 2 * HD, N), F32), V((2, 2, 8, N), F32), V((2, QD, N), BF), V((2, 8, N), F32),
             V((2, HD, N), BF), V((2, N, FF), BF), V((2, N, FF), BF),
             V((2, N, QD), BF), V((2 * R, D), F32), V((2 * R, D), BF), V((R, D), BF),
             V((2, 2 * R, D), BF), V((2, R, D), BF),
             V((N, N), BF), V((N, N), BF), V((HD, N), BF), V((QD, N), BF),
             V((2, R, D), BF), V((2, R, D), BF), V((R, D), BF), V((R, D), BF),
+            V((2, G, D), BF), V((2, 8, D), F32), V((2, HEAD, 128), F32),
             dma((6,)), dma((6,)), dma((2, 6)),
             dma((2, 4, 3)), dma((2, 4, 3)), dma((2, 4, 2)), dma((2, 4, 2)), dma((2,)), dma((2,)),
-        ],
+        ] + extra,
         name="layers",
         compiler_params=pltpu.CompilerParams(
             collective_id=0, has_side_effects=True, vmem_limit_bytes=63 * 2**20
@@ -417,19 +619,19 @@
     qk_gain = jnp.concatenate([query_gain[0], key_gain[0]], axis=0).astype(F32).T
     qk_gain = jnp.pad(qk_gain, ((0, 0), (0, 128 - 2 * NH)))
     wq = qkv_weight[0].reshape(D, 3 * HD).T
-    y, ig, gq, go, gu, gd, gg, gh = fused(
-        x, ct, seg[:, None], seg[None, :], small, qk_gain, wq, out_weight[0], up_weight[0], down_weight[0]
+    chain = lax.axis_size("batch") == 4
+    y, ig, g, gg, gh = fused(
+        chain, x, ct, seg[:, None], seg[None, :], small, qk_gain, wq, out_weight[0], up_weight[0],
+        down_weight[0],
     )
-
-    def reduced(g):
+    if not chain:
         theirs = lax.ppermute(g[1 - s], "section", [(0, 1), (1, 0)])
-        both = (g[s].astype(F32) + theirs.astype(F32)).astype(g.dtype)
-        return both
-
-    big = [reduced(g) for g in (gq, go, gu, gd)]
-    gq, go, gu, gd = lax.psum(tuple(big), "batch")
-    gg = lax.psum(gg[:, :2], ("section", "batch", "tensor"))[s]
-    gh = lax.psum(gh[..., 0], ("section", "batch"))[s]
+        g = lax.psum((g[s].astype(F32) + theirs.astype(F32)).astype(BF), "batch")
+        gg = lax.psum(gg, ("section", "batch", "tensor"))[s]
+        gh = lax.psum(gh, ("section", "batch"))[s]
+    FF = up_weight.shape[2]
+    gd, gu, go, gq = (g[:FF], g[FF : FF + D], g[FF + D : FF + D + HD], g[FF + D + HD :])
+    gh = gh[:, : 2 * NH].T.reshape(2, NH, HEAD)
     return (
         y[:, :own][None],
         ig[:, :own][None],

time: 539 us -> 422 us (0.78)
  waiting for transfers between devices: 140 us -> 0 us
  Pallas kernels: 290 us -> 397 us
  blocking collectives: 64.4 us -> 0 us
  between operations: 14.2 us -> 0.71 us
    pallas_call x1, Pallas kernels: 290 us -> 397 us  [fused(): pl.pallas_call(functools.partial(body, chain), out_shape=(shape((2, R, D)...]
    ppermute x4 -> x0, waiting for transfers between devices: 73 us -> none  [reduced(): theirs = lax.ppermute(g[1 - s], 'section', [(0, 1), (1, 0)])]
    psum x1 -> x0, waiting for transfers between devices: 67.3 us -> none  [shards(): gq, go, gu, gd = lax.psum(tuple(big), 'batch')]
    psum x2 -> x0, blocking collectives: 64.4 us -> none  [the longest x1 42.5 us: shards(): gg = lax.psum(gg[:, :2], ('section', 'batch', 'tensor'))[s]]
  transfers between devices with their start and end apart: 5 -> 0, of which waited for: 2 -> 0; matrix products, arithmetic and copies ran while one was open for 1% -> 0% of each run, Pallas kernels for 0% -> 0%
where the time goes in v2:
time: 422 us
  Pallas kernels  397 us (94%)
  local copies, waits for them, and re-layouts  15.6 us (4%)
  other arithmetic  8.71 us (2%)
    pallas_call x1, Pallas kernels, fused(): pl.pallas_call(functools.partial(body, chain), out_shape=(shape((2, R, D)...  397 us

profile of v2, /device:TPU:0, one launch (start us, length us, event | category | flops | bytes accessed | tf_op | source)
XLA Modules:
  0.0 421.6 jit_solution(843499775545035517)
XLA Ops:
  0.7 0.7 copy-done
  1.3 0.7 pad_maximum_fusion
  2.0 0.7 convert_element_type.20
  2.7 0.1 copy.47
  2.8 0.6 pad_convert_fusion.qkg_in
  3.5 0.7 pad_convert_fusion.1
  4.4 0.1 reduce.4
  4.5 0.1 convert_reduce_fusion
  4.8 0.7 broadcast_in_dim_reshape.13.segr_ref
  5.4 1.0 broadcast_in_dim_reshape.18.segc_ref
  6.4 1.1 dynamic-slice_bitcast_fusion
  7.5 0.7 pad.24.ct_ref
  8.3 0.7 pad.23.x_ref
  9.0 396.5 %layers.1 = (bf16[2,208,768]{2,1,0:T(8,128)(2,1)}, f32[2,208,768]{2,1,0:T(8,128)}, bf16[2304,768]{1,0:T(8,128)(2,1)}, f32[8,768]{1,0:T(8,128)}, f32[64,128]{1,0:T(8,128)}) custom-call(bf16[208,768]{1,0:T(8,128)(2,1)} %pad.23.x_ref, bf16[208,768]{1,0:T(8,128)(2,1)} %pad.24.ct_ref, s32[832,1]{1,0:T(8,128)} %broadcast_in_dim_reshape.18.segc_ref, ...), custom_call_target="tpu_custom_call" | custom-call | tf_op jit(solution)/shard_map/layers/pallas_call | solution.py:565
  405.6 1.9 slice_bitcast_fusion.1
  407.5 1.4 fusion.1
  408.9 0.8 slice_bitcast_fusion.4
  409.7 0.7 slice_bitcast_fusion.2
  410.4 1.8 copy.50
  412.1 1.4 copy.49
  413.5 1.8 bitcast_convert_fusion.2
  415.3 2.4 slice_bitcast_fusion
  417.7 1.3 slice_convert_fusion
  419.1 2.5 bitcast_convert_fusion
  (13 shorter events, 0.4 us)
Async XLA Ops:
  0.6 0.7 copy-start
  4.2 4.8 %copy-start.2 = (f32[8,768]{1,0:T(8,128)}, f32[8,768]{1,0:T(8,128)S(1)}, u32[]{:S(2)}) copy-start(f32[8,768]{1,0:T(8,128)S(1)} %scatter.14.sml_in) | copy-start | bytes 73732
  409.7 8.1 %copy-start.1 = (bf16[2304,768]{1,0:T(8,128)(2,1)S(1)}, bf16[2304,768]{1,0:T(8,128)(2,1)}, u32[]{:S(2)}) copy-start(bf16[2304,768]{1,0:T(8,128)(2,1)} %get-tuple-element.42) | copy-start | bytes 10616836

commit v3 on v2

--- a/solution.py
+++ b/solution.py
@@ -15,12 +15,19 @@
 KEY_BLOCK = 64
 COLS = 256
 SUB = 192
+CHUNKS = 2
 TAKEN = ((0, 0, 0, 1, 2, 3, 5, 7, 9, 10, 11, 12), (2, 3, 4, 6, 7, 9, 10, 11, 12, 12, 12, 12))
 LAYER_POINTS = 7
 
 
 def ceil_to(n, m):
     return -(-n // m) * m
+
+
+def chunks_of(rows):
+    step = max(32, rows // CHUNKS // 32 * 32)
+    starts = [i * step for i in range(CHUNKS) if i * step < rows]
+    return [(a, b - a) for a, b in zip(starts, starts[1:] + [rows])]
 
 
 def mm(a, b):
@@ -58,7 +65,7 @@
     e_buf, d_buf, dot_buf, dqkv_t,
     ybuf, dxbuf, ylo, dxlo,
     grads, gains, hgains,
-    w_loc, w_send, w_recv, ag_s, ag_r, rs_s, rs_r, x_s, x_r,
+    w_loc, w_send, w_recv, wz_s, wz_r, ag_s, ag_r, rs_s, rs_r, x_s, x_r,
     gx, gz, gpart, gfin, gains_x, hgains_x, gains_z, hgains_z, gains_t,
     gx_s, gx_r, gz_s, gz_r, g_loc, sm_s, sm_r,
 ):
@@ -75,8 +82,14 @@
     NB = N // KEY_BLOCK
     pos = c * 2 + y
     ypos = c * 2 + 1 - y
-    own_rows = pl.ds(pl.multiple_of(pos * R, 16), R)
-    y_rows = pl.ds(pl.multiple_of(ypos * R, 16), R)
+    CH = chunks_of(R)
+
+    def block_rows(k, at):
+        off, n = CH[k]
+        return pl.ds(pl.multiple_of(4 * off + at * n, 16), n)
+
+    def own_rows(k):
+        return pl.ds(CH[k][0], CH[k][1])
 
     diag_id = (s, b, (1 - y) * 2 + 1 - c)
     z_ids = [(s, lax.rem(b + k, 4), t) for k in (1, 2, 3)] if chain else []
@@ -94,66 +107,129 @@
         pltpu.make_async_copy(ref, ref, sem).wait()
 
     moves = ((sml_in, sml), (qkg_in, qkg), (wq_in, wq), (wo_in, wo), (wu_in, wu), (wd_in, wd))
+    pair_id = (s, b + 1 - 2 * lax.rem(b, 2), t)
+    near = lax.rem(b, 2)
+    blocks = []
+    for i in range(2, 6):
+        rows = moves[i][0].shape[0]
+        step = min(rows, 2 * SUB if i > 3 else SUB)
+        blocks += [(i, at, step) for at in range(0, rows, step)]
+
+    def half_block(ref, j, h):
+        _, at, n = blocks[j]
+        return ref.at[pl.ds(pl.multiple_of(at + h * (n // 2), 16), n // 2)]
+
+    def send_block(j):
+        src, dst = moves[blocks[j][0]]
+        if chain:
+            remote(half_block(src, j, near), half_block(dst.at[s], j, near), w_send.at[j], w_recv.at[j], x_id).start()
+        else:
+            _, at, n = blocks[j]
+            remote(src.at[at : at + n], dst.at[s, at : at + n], w_send.at[j], w_recv.at[j], x_id).start()
+
+    def forward_blocks(lo, hi):
+        if chain:
+            for j in range(lo, hi):
+                got = half_block(moves[blocks[j][0]][1].at[1 - s], j, near)
+                arrived(got, w_recv.at[j])
+                remote(got, got, wz_s.at[j], wz_r.at[j], pair_id).start()
+
     for i, (src, dst) in enumerate(moves):
-        remote(src, dst.at[s], w_send.at[i], w_recv.at[s, i], x_id).start()
+        if i < 2:
+            remote(src, dst.at[s], w_send.at[len(blocks) + i], w_recv.at[len(blocks) + i], x_id).start()
+        else:
+            for j in range(len(blocks)):
+                if blocks[j][0] == i:
+                    send_block(j)
         pltpu.make_async_copy(src, dst.at[s], w_loc.at[i]).start()
-    for i, (src, dst) in enumerate(moves):
-        pltpu.make_async_copy(src, dst.at[s], w_loc.at[i]).wait()
 
     def weights_here(l, i):
+        src, dst = moves[i]
+
+        @pl.when(l == s)
+        def _():
+            pltpu.make_async_copy(src, dst.at[s], w_loc.at[i]).wait()
+
         @pl.when(l != s)
         def _():
-            arrived(moves[i][1].at[1 - s], w_recv.at[1 - s, i])
-
-    def gather_start(buf, l, op):
-        part_of = l if op < 2 else 0
-        mine = buf.at[part_of, own_rows]
-        remote(mine, mine, ag_s.at[l, op, 0], ag_r.at[l, op, 0], core_id).start()
-        remote(mine, mine, ag_s.at[l, op, 1], ag_r.at[l, op, 1], y_id).start()
-
-    def gather_finish(buf, l, op):
-        part_of = l if op < 2 else 0
-        mine = buf.at[part_of, own_rows]
-        theirs = buf.at[part_of, y_rows]
-        arrived(theirs, ag_r.at[l, op, 1])
-        third = remote(theirs, theirs, ag_s.at[l, op, 2], ag_r.at[l, op, 2], core_id)
-        third.start()
-        arrived(mine, ag_r.at[l, op, 0])
-        arrived(mine, ag_r.at[l, op, 2])
-        arrived(mine, ag_s.at[l, op, 0])
-        arrived(mine, ag_s.at[l, op, 1])
-        arrived(theirs, ag_s.at[l, op, 2])
-
-    def scatter_start(product, l, op):
+            if i < 2:
+                arrived(dst.at[1 - s], w_recv.at[len(blocks) + i])
+            for j in range(len(blocks)):
+                if blocks[j][0] == i:
+                    if chain:
+                        arrived(half_block(dst.at[1 - s], j, 1 - near), wz_r.at[j])
+                    else:
+                        _, at, n = blocks[j]
+                        arrived(dst.at[1 - s, at : at + n], w_recv.at[j])
+
+    def finish_weights():
+        for i in range(2):
+            arrived(moves[i][1].at[s], w_send.at[len(blocks) + i])
+        for j in range(len(blocks)):
+            i, at, n = blocks[j]
+            if chain:
+                arrived(half_block(moves[i][1].at[s], j, near), w_send.at[j])
+                arrived(half_block(moves[i][1].at[1 - s], j, near), wz_s.at[j])
+            else:
+                arrived(moves[i][1].at[s, at : at + n], w_send.at[j])
+
+    def gather_start(buf, slot, l, op, k):
+        mine = buf.at[slot, block_rows(k, pos)]
+        remote(mine, mine, ag_s.at[l, op, 0, k], ag_r.at[l, op, 0, k], core_id).start()
+        remote(mine, mine, ag_s.at[l, op, 1, k], ag_r.at[l, op, 1, k], y_id).start()
+
+    def gather_pass(buf, slot, l, op, k):
+        theirs = buf.at[slot, block_rows(k, ypos)]
+        arrived(theirs, ag_r.at[l, op, 1, k])
+        remote(theirs, theirs, ag_s.at[l, op, 2, k], ag_r.at[l, op, 2, k], core_id).start()
+
+    def gather_finish(buf, slot, l, op, k):
+        mine = buf.at[slot, block_rows(k, pos)]
+        arrived(mine, ag_r.at[l, op, 0, k])
+        arrived(mine, ag_r.at[l, op, 2, k])
+        arrived(mine, ag_s.at[l, op, 0, k])
+        arrived(mine, ag_s.at[l, op, 1, k])
+        arrived(mine, ag_s.at[l, op, 2, k])
+
+    def pair_rows(k):
+        return pl.ds(2 * CH[k][0], 2 * CH[k][1])
+
+    def scatter_start(product, l, op, k):
         slot = op % 2
+        off, n = CH[k]
 
         def send_tile(j, carry):
             cols = pl.ds(pl.multiple_of(j * COLS, COLS), COLS)
-            sendbuf[:, cols] = product(pl.multiple_of((1 - c) * 2 * R, 16), cols).astype(BF)
+            at = pl.ds(pl.multiple_of(4 * off + (1 - c) * 2 * n, 16), 2 * n)
+            sendbuf[pair_rows(k), cols] = product(at, cols).astype(BF)
             return carry
 
         lax.fori_loop(0, D // COLS, send_tile, 0)
-        first = remote(sendbuf, crecv.at[slot], rs_s.at[l, op, 0], rs_r.at[l, op, 0], core_id)
-        first.start()
+        mine = sendbuf.at[pair_rows(k)]
+        remote(mine, crecv.at[slot, pair_rows(k)], rs_s.at[l, op, 0, k], rs_r.at[l, op, 0, k], core_id).start()
 
         def own_tile(j, carry):
             cols = pl.ds(pl.multiple_of(j * COLS, COLS), COLS)
-            part[:, cols] = product(pl.multiple_of(c * 2 * R, 16), cols)
+            at = pl.ds(pl.multiple_of(4 * off + c * 2 * n, 16), 2 * n)
+            part[pair_rows(k), cols] = product(at, cols)
             return carry
 
         lax.fori_loop(0, D // COLS, own_tile, 0)
-        arrived(sendbuf, rs_r.at[l, op, 0])
-        other = pl.ds(pl.multiple_of((1 - y) * R, 16), R)
-        ysend[...] = (part[other] + crecv[slot, other].astype(F32)).astype(BF)
-        remote(ysend, yrecv.at[slot], rs_s.at[l, op, 1], rs_r.at[l, op, 1], y_id).start()
-
-    def scatter_finish(l, op):
+        arrived(mine, rs_r.at[l, op, 0, k])
+        other = pl.ds(pl.multiple_of(2 * off + (1 - y) * n, 16), n)
+        ysend[own_rows(k)] = (part[other] + crecv[slot, other].astype(F32)).astype(BF)
+        remote(
+            ysend.at[own_rows(k)], yrecv.at[slot, own_rows(k)], rs_s.at[l, op, 1, k], rs_r.at[l, op, 1, k], y_id
+        ).start()
+
+    def scatter_finish(l, op, k):
         slot = op % 2
-        mine = pl.ds(pl.multiple_of(y * R, 16), R)
-        arrived(sendbuf, rs_s.at[l, op, 0])
-        arrived(ysend, rs_s.at[l, op, 1])
-        arrived(ysend, rs_r.at[l, op, 1])
-        return part[mine] + crecv[slot, mine].astype(F32) + yrecv[slot].astype(F32)
+        off, n = CH[k]
+        mine = pl.ds(pl.multiple_of(2 * off + y * n, 16), n)
+        arrived(sendbuf.at[pair_rows(k)], rs_s.at[l, op, 0, k])
+        arrived(ysend.at[own_rows(k)], rs_s.at[l, op, 1, k])
+        arrived(ysend.at[own_rows(k)], rs_r.at[l, op, 1, k])
+        return part[mine] + crecv[slot, mine].astype(F32) + yrecv[slot, own_rows(k)].astype(F32)
 
     FD, UP, OUT = 0, FF, FF + D
     QKV = OUT + HD
@@ -282,46 +358,41 @@
     def q_rows(h):
         return pl.ds(pl.multiple_of(h * HEAD, HEAD), HEAD)
 
-    def forward(l):
-        weights_here(l, 0)
-        weights_here(l, 1)
-        xh, r = normed(xres[...])
-        xh1[l] = xh
-        r1[l] = r
-        a_all[l, own_rows] = (xh * sml[l, 0:1]).astype(BF)
-        gather_start(a_all, l, 0)
-        weights_here(l, 2)
-        gather_finish(a_all, l, 0)
-
-        def project(i, carry):
-            rows = pl.ds(pl.multiple_of(i * HD, HEAD), HD)
-            qkvb[l, rows] = mm_nt(wq[l, rows], a_all[l]).astype(BF)
-            return carry
-
-        def project_normed(i, carry):
-            rows = pl.ds(pl.multiple_of(i * HD, HEAD), HD)
-            v = mm_nt(wq[l, rows], a_all[l])
+    def attention_input(l, k):
+        xh, r = normed(xres[own_rows(k)])
+        xh1[l, own_rows(k)] = xh
+        r1[l, own_rows(k)] = r
+        a_all[l, block_rows(k, pos)] = (xh * sml[l, 0:1]).astype(BF)
+        gather_start(a_all, l, l, 0, k)
+
+    def project(l, k):
+        off, n = CH[k]
+        rows, lanes = slice(4 * off, 4 * (off + n)), slice(4 * off, 4 * (off + n))
+
+        def query_key(i, carry):
+            at = pl.ds(pl.multiple_of(i * HD, HEAD), HD)
+            v = mm_nt(wq[l, at], a_all[l, rows])
             for h in range(NH):
                 u = v[h * HEAD : (h + 1) * HEAD]
                 u = u - jnp.mean(u, axis=0, keepdims=True)
                 rr = lax.rsqrt(jnp.mean(u * u, axis=0, keepdims=True) + EPS)
                 u = u * rr
                 at = pl.ds(pl.multiple_of(i * HD + h * HEAD, HEAD), HEAD)
-                qkh[l, at] = u
-                qkr[l, i, pl.ds(h, 1)] = rr
+                qkh[l, at, lanes] = u
+                qkr[l, i, pl.ds(h, 1), lanes] = rr
                 scale = jnp.where(i == 0, HEAD**-0.5, 1.0).astype(F32)
                 gain = jnp.where(i == 0, qkg[l, :, h : h + 1], qkg[l, :, NH + h : NH + h + 1])
-                qkvb[l, at] = ((u * gain).astype(BF).astype(F32) * scale).astype(BF)
-            return carry
-
-        lax.fori_loop(0, 2, project_normed, 0)
-        project(2, 0)
-
+                qkvb[l, at, lanes] = ((u * gain).astype(BF).astype(F32) * scale).astype(BF)
+            return carry
+
+        lax.fori_loop(0, 2, query_key, 0)
+        qkvb[l, 2 * HD :, lanes] = mm_nt(wq[l, 2 * HD :], a_all[l, rows]).astype(BF)
+
+    def attention(l):
         def head(h, carry):
             q_t = qkvb[l, q_rows(h)]
-            k_rows = qkvb[l, q_rows(NH + h)].astype(F32).T.astype(BF)
             v_t = qkvb[l, q_rows(2 * NH + h)]
-            rows_buf[0, :, :HEAD] = k_rows
+            rows_buf[0, :, :HEAD] = qkvb[l, q_rows(NH + h)].astype(F32).T.astype(BF)
 
             def block(i, total):
                 at = pl.ds(pl.multiple_of(i * KEY_BLOCK, KEY_BLOCK), KEY_BLOCK)
@@ -337,21 +408,13 @@
 
         lax.fori_loop(0, NH, head, 0)
         rows_buf[1, :, :HD] = o_t[l].astype(F32).T.astype(BF)
-        weights_here(l, 3)
-        scatter_start(lambda at, cols: mm(rows_buf[1, pl.ds(at, 2 * R), :HD], wo[l, :, cols]), l, 0)
-        residual = xres[...] + scatter_finish(l, 0)
-        xres[...] = residual
-        xh, r = normed(residual)
-        xh2[l] = xh
-        r2[l] = r
-        b_all[l, own_rows] = (xh * sml[l, 1:2]).astype(BF)
-        gather_start(b_all, l, 1)
-        weights_here(l, 4)
-        gather_finish(b_all, l, 1)
-
-        def hidden(i, carry):
-            rows = pl.ds(pl.multiple_of(lax.rem(i, 4) * R, 16), R)
-            cols = pl.ds(pl.multiple_of((i // 4) * COLS, COLS), COLS)
+
+    def hidden(l, k):
+        off, n = CH[k]
+
+        def tile(i, carry):
+            rows = pl.ds(pl.multiple_of(4 * off + lax.rem(i, 2) * 2 * n, 16), 2 * n)
+            cols = pl.ds(pl.multiple_of((i // 2) * COLS, COLS), COLS)
             u = mm(b_all[l, rows], wu[l, :, cols])
             cdf = 0.5 * (1.0 + lax.erf(u * 0.7071067811865476))
             pdf = jnp.exp(-0.5 * u * u) * 0.3989422804014327
@@ -359,68 +422,47 @@
             gp_all[l, rows, cols] = (cdf + u * pdf).astype(BF)
             return carry
 
-        lax.fori_loop(0, 4 * (FF // COLS), hidden, 0)
-        weights_here(l, 5)
-        scatter_start(lambda at, cols: mm(g_all[l, pl.ds(at, 2 * R)], wd[l, :, cols]), l, 1)
-        out = xres[...] + scatter_finish(l, 1)
-        rounded = out.astype(BF)
-        ybuf[l] = rounded
-        xres[...] = rounded.astype(F32)
-
-    xres[...] = x_ref[...].astype(F32)
-
-    def forward_step(l, carry):
-        forward(l)
-        return carry
-
-    lax.fori_loop(0, 2, forward_step, 0)
-    y_move = remote(ybuf.at[1 - s], ylo, x_s.at[0], x_r.at[0], x_id)
-    y_move.start()
-
-    def backward(l):
-        live = l == 0
-        dm_all[0, own_rows] = xres[...].astype(BF)
-        gather_start(dm_all, l, 2)
-        progress(0, live)
-        gather_finish(dm_all, l, 2)
-
-        def hidden(i, carry):
-            rows = pl.ds(pl.multiple_of(lax.rem(i, 4) * R, 16), R)
-            cols = pl.ds(pl.multiple_of((i // 4) * COLS, COLS), COLS)
+        lax.fori_loop(0, 2 * (FF // COLS), tile, 0)
+
+    def hidden_back(l, k):
+        off, n = CH[k]
+
+        def tile(i, carry):
+            rows = pl.ds(pl.multiple_of(4 * off + lax.rem(i, 2) * 2 * n, 16), 2 * n)
+            cols = pl.ds(pl.multiple_of((i // 2) * COLS, COLS), COLS)
             dg = mm_nt(dm_all[0, rows], wd[l, cols])
             gp_all[l, rows, cols] = (dg * gp_all[l, rows, cols].astype(F32)).astype(BF)
             return carry
 
-        lax.fori_loop(0, 4 * (FF // COLS), hidden, 0)
-        progress(1, live)
-        scatter_start(lambda at, cols: mm_nt(gp_all[l, pl.ds(at, 2 * R)], wu[l, cols]), l, 2)
-
-        def hidden_grads(i, carry):
+        lax.fori_loop(0, 2 * (FF // COLS), tile, 0)
+
+    def down_grad(l):
+        def tile(i, carry):
             cols = pl.ds(pl.multiple_of(i * COLS, COLS), COLS)
-            grads[l, pl.ds(pl.multiple_of(FD + i * COLS, COLS), COLS)] = mm_tn(
-                g_all[l, :, cols], dm_all[0]
-            ).astype(BF)
-            grads[l, pl.ds(pl.multiple_of(UP + i * COLS, COLS), COLS)] = mm_tn(
-                b_all[l, :, cols], gp_all[l]
-            ).astype(BF)
-            return carry
-
-        lax.fori_loop(0, FF // COLS, hidden_grads, 0)
-        send_grads(l, 0, OUT // SUB)
-        progress(2, live)
-        db = scatter_finish(l, 2)
-        gains[l, 1:2] = jnp.sum(db * xh2[l], axis=0, keepdims=True)
-        dh = xres[...] + normed_back(db, sml[l, 1:2], xh2[l], r2[l])
-        xres[...] = dh
-        da_all[0, own_rows] = dh.astype(BF)
-        gather_start(da_all, l, 3)
-        progress(3, live)
-        gather_finish(da_all, l, 3)
-        dot_buf[...] = mm_nt(wo[l], da_all[0]).astype(BF)
-        grads[l, OUT:QKV] = mm(o_t[l], da_all[0]).astype(BF)
-        send_grads(l, OUT // SUB, QKV // SUB)
-        progress(4, live)
-
+            at = pl.ds(pl.multiple_of(FD + i * COLS, COLS), COLS)
+            grads[l, at] = mm_tn(g_all[l, :, cols], dm_all[0]).astype(BF)
+            return carry
+
+        lax.fori_loop(0, FF // COLS, tile, 0)
+        send_grads(l, 0, UP // SUB)
+
+    def up_grad(l):
+        def tile(i, carry):
+            cols = pl.ds(pl.multiple_of(i * COLS, COLS), COLS)
+            at = pl.ds(pl.multiple_of(UP + i * COLS, COLS), COLS)
+            grads[l, at] = mm_tn(b_all[l, :, cols], gp_all[l]).astype(BF)
+            return carry
+
+        lax.fori_loop(0, D // COLS, tile, 0)
+        send_grads(l, UP // SUB, OUT // SUB)
+
+    def gains_of(l, i, h):
+        out = qkg[l, :, i * NH : i * NH + 1]
+        for k in range(1, NH):
+            out = jnp.where(h == k, qkg[l, :, i * NH + k : i * NH + k + 1], out)
+        return out
+
+    def attention_back(l):
         def head(h, carry):
             q_t = qkvb[l, q_rows(h)]
             k_t = qkvb[l, q_rows(NH + h)]
@@ -450,38 +492,147 @@
                 uh = qkh[l, at]
                 lanes = lax.broadcasted_iota(jnp.int32, (HEAD, 128), 1) == i * NH + h
                 hgains[l] = jnp.where(lanes, jnp.sum(dv * uh, axis=1, keepdims=True), hgains[l])
-                gain = gains_of(l, i, h)
-                g = dv * gain
+                g = dv * gains_of(l, i, h)
                 back = g - jnp.mean(g, axis=0, keepdims=True) - uh * jnp.mean(g * uh, axis=0, keepdims=True)
                 dqkv_t[at] = (qkr[l, i, pl.ds(h, 1)] * back).astype(BF)
             return carry
 
-        def gains_of(l, i, h):
-            out = qkg[l, :, i * NH : i * NH + 1]
-            for k in range(1, NH):
-                out = jnp.where(h == k, qkg[l, :, i * NH + k : i * NH + k + 1], out)
-            return out
-
         hgains[l] = jnp.zeros((HEAD, 128), F32)
-        gains[l] = jnp.where(lax.broadcasted_iota(jnp.int32, (8, D), 0) == 1, gains[l], 0.0)
         lax.fori_loop(0, NH, head, 0)
-        progress(5, live)
         rows_buf[0] = dqkv_t[...].astype(F32).T.astype(BF)
-        scatter_start(lambda at, cols: mm(rows_buf[0, pl.ds(at, 2 * R)], wq[l, :, cols]), l, 3)
+
+    each = range(len(CH))
+    gains[...] = jnp.zeros_like(gains)
+
+    for l in range(2):
+        if l == 0:
+            weights_here(l, 0)
+            weights_here(l, 1)
+            for k in each:
+                xres[own_rows(k)] = x_ref[own_rows(k)].astype(F32)
+                attention_input(l, k)
+                dm_all[0, block_rows(k, pos)] = ct_ref[own_rows(k)]
+            forward_blocks(0, 3)
+        else:
+            weights_here(l, 1)
+        weights_here(l, 2)
+        for k in each:
+            gather_pass(a_all, l, l, 0, k)
+        for k in each:
+            gather_finish(a_all, l, l, 0, k)
+            project(l, k)
+        if l == 0:
+            for k in each:
+                gather_start(dm_all, 0, 1, 2, k)
+            forward_blocks(3, 4)
+        attention(l)
+        if l == 0:
+            forward_blocks(4, 6)
+            for k in each:
+                gather_pass(dm_all, 0, 1, 2, k)
+        weights_here(l, 3)
+        for k in each:
+            scatter_start(lambda at, cols: mm(rows_buf[1, at, :HD], wo[l, :, cols]), l, 0, k)
+        for k in each:
+            residual = xres[own_rows(k)] + scatter_finish(l, 0, k)
+            xres[own_rows(k)] = residual
+            xh, r = normed(residual)
+            xh2[l, own_rows(k)] = xh
+            r2[l, own_rows(k)] = r
+            b_all[l, block_rows(k, pos)] = (xh * sml[l, 1:2]).astype(BF)
+            gather_start(b_all, l, l, 1, k)
+        if l == 0:
+            forward_blocks(6, len(blocks))
+        weights_here(l, 4)
+        weights_here(l, 5)
+        gather_pass(b_all, l, l, 1, 0)
+        for k in each:
+            gather_finish(b_all, l, l, 1, k)
+            hidden(l, k)
+            if k + 1 < len(CH):
+                gather_pass(b_all, l, l, 1, k + 1)
+            scatter_start(lambda at, cols: mm(g_all[l, at], wd[l, :, cols]), l, 1, k)
+        if l == 0:
+            for k in each:
+                rounded = (xres[own_rows(k)] + scatter_finish(l, 1, k)).astype(BF)
+                ybuf[l, own_rows(k)] = rounded
+                xres[own_rows(k)] = rounded.astype(F32)
+                if k == 0:
+                    weights_here(1, 0)
+                attention_input(1, k)
+
+    for l in (1, 0):
+        if l == 1:
+            for k in each:
+                gather_finish(dm_all, 0, l, 2, k)
+                hidden_back(l, k)
+            down_grad(l)
+            for k in each:
+                ybuf[l, own_rows(k)] = (xres[own_rows(k)] + scatter_finish(l, 1, k)).astype(BF)
+                xres[own_rows(k)] = ct_ref[own_rows(k)].astype(F32)
+            y_move = remote(ybuf.at[1 - s], ylo, x_s.at[0], x_r.at[0], x_id)
+            y_move.start()
+            for k in each:
+                scatter_start(lambda at, cols: mm_nt(gp_all[l, at], wu[l, cols]), l, 2, k)
+        else:
+            progress(0, True)
+            gather_pass(dm_all, 0, l, 2, 0)
+            for k in each:
+                gather_finish(dm_all, 0, l, 2, k)
+                hidden_back(l, k)
+                if k + 1 < len(CH):
+                    gather_pass(dm_all, 0, l, 2, k + 1)
+                scatter_start(lambda at, cols: mm_nt(gp_all[l, at], wu[l, cols]), l, 2, k)
+            down_grad(l)
+            progress(1, True)
+        up_grad(l)
+        if l == 0:
+            progress(2, True)
+        for k in each:
+            db = scatter_finish(l, 2, k)
+            xh = xh2[l, own_rows(k)]
+            gains[l, 1:2] = gains[l, 1:2] + jnp.sum(db * xh, axis=0, keepdims=True)
+            dh = xres[own_rows(k)] + normed_back(db, sml[l, 1:2], xh, r2[l, own_rows(k)])
+            xres[own_rows(k)] = dh
+            da_all[0, block_rows(k, pos)] = dh.astype(BF)
+            gather_start(da_all, 0, l, 3, k)
+        if l == 0:
+            progress(3, True)
+        for k in each:
+            gather_pass(da_all, 0, l, 3, k)
+        for k in each:
+            gather_finish(da_all, 0, l, 3, k)
+        dot_buf[...] = mm_nt(wo[l], da_all[0]).astype(BF)
+        grads[l, OUT:QKV] = mm(o_t[l], da_all[0]).astype(BF)
+        send_grads(l, OUT // SUB, QKV // SUB)
+        if l == 0:
+            progress(4, True)
+        attention_back(l)
+        if l == 0:
+            progress(5, True)
+        for k in each:
+            scatter_start(lambda at, cols: mm(rows_buf[0, at], wq[l, :, cols]), l, 3, k)
         grads[l, QKV:] = mm(dqkv_t[...], a_all[l]).astype(BF)
         send_grads(l, QKV // SUB, KS)
-        progress(6, live)
-        da = scatter_finish(l, 3)
-        gains[l, 0:1] = jnp.sum(da * xh1[l], axis=0, keepdims=True)
-        dx = xres[...] + normed_back(da, sml[l, 0:1], xh1[l], r1[l])
-        rounded = dx.astype(BF)
-        dxbuf[l] = rounded
-        kept = jnp.where(l == 0, dx, rounded.astype(F32))
-        xres[...] = rounded.astype(F32)
+        if l == 0:
+            progress(6, True)
+        for k in each:
+            da = scatter_finish(l, 3, k)
+            xh = xh1[l, own_rows(k)]
+            gains[l, 0:1] = gains[l, 0:1] + jnp.sum(da * xh, axis=0, keepdims=True)
+            dx = xres[own_rows(k)] + normed_back(da, sml[l, 0:1], xh, r1[l, own_rows(k)])
+            rounded = dx.astype(BF)
+            dxbuf[l, own_rows(k)] = rounded
+            if l == 1:
+                xres[own_rows(k)] = rounded.astype(F32)
+                dm_all[0, block_rows(k, pos)] = rounded
+                gather_start(dm_all, 0, 0, 2, k)
+            else:
+                xres[own_rows(k)] = dx
 
         @pl.when(l == s)
         def _():
-            ig_out[s] = kept
+            ig_out[s] = dxbuf[1].astype(F32) if l == 1 else xres[...]
 
         @pl.when(l != s)
         def _():
@@ -490,13 +641,6 @@
                 remote(gains.at[1 - s], gains_x, sm_s.at[0], sm_r.at[0], x_id).start()
                 remote(hgains.at[1 - s], hgains_x, sm_s.at[1], sm_r.at[1], x_id).start()
 
-    xres[...] = ct_ref[...].astype(F32)
-
-    def backward_step(i, carry):
-        backward(1 - i)
-        return carry
-
-    lax.fori_loop(0, 2, backward_step, 0)
     progress(LAYER_POINTS, True)
     if chain:
         arrived(gains_x, sm_r.at[0])
@@ -527,8 +671,7 @@
     y_move.wait()
     y_out[s] = ybuf[s]
     y_out[1 - s] = ylo[...]
-    for i, (src, dst) in enumerate(moves):
-        arrived(dst.at[s], w_send.at[i])
+    finish_weights()
     arrived(dxlo, x_s.at[1])
     arrived(dxlo, x_r.at[1])
     ig_out[1 - s] = dxlo[...].astype(F32)
@@ -547,6 +690,7 @@
     N = 4 * R
     QD, HD, FF = wq.shape[0], wo.shape[0], wu.shape[1]
     NH = HD // HEAD
+    CH = len(chunks_of(R))
     vmem = pl.BlockSpec(memory_space=pltpu.VMEM)
     hbm = pl.BlockSpec(memory_space=pl.ANY)
     shape = jax.ShapeDtypeStruct
@@ -585,8 +729,8 @@
             V((N, N), BF), V((N, N), BF), V((HD, N), BF), V((QD, N), BF),
             V((2, R, D), BF), V((2, R, D), BF), V((R, D), BF), V((R, D), BF),
             V((2, G, D), BF), V((2, 8, D), F32), V((2, HEAD, 128), F32),
-            dma((6,)), dma((6,)), dma((2, 6)),
-            dma((2, 4, 3)), dma((2, 4, 3)), dma((2, 4, 2)), dma((2, 4, 2)), dma((2,)), dma((2,)),
+            dma((6,)), dma((16,)), dma((16,)), dma((16,)), dma((16,)),
+            dma((2, 4, 3, CH)), dma((2, 4, 3, CH)), dma((2, 4, 2, CH)), dma((2, 4, 2, CH)), dma((2,)), dma((2,)),
         ] + extra,
         name="layers",
         compiler_params=pltpu.CompilerParams(
@@ -614,7 +758,8 @@
     places = jnp.arange(seq_len, dtype=jnp.int32)
     seg = jnp.sum((places[:, None] >= bounds[None, :]).astype(jnp.int32), axis=-1)
     seg = seg.reshape(2, 2, own).transpose(1, 0, 2).reshape(4, own)
-    seg = jnp.pad(seg, ((0, 0), (0, R - own)), constant_values=-1).reshape(N)
+    seg = jnp.pad(seg, ((0, 0), (0, R - own)), constant_values=-1)
+    seg = jnp.concatenate([seg[:, a : a + n].reshape(4 * n) for a, n in chunks_of(R)])
     small = jnp.zeros((8, D), F32).at[0].set(attn_gain[0].astype(F32)).at[1].set(mlp_gain[0].astype(F32))
     qk_gain = jnp.concatenate([query_gain[0], key_gain[0]], axis=0).astype(F32).T
     qk_gain = jnp.pad(qk_gain, ((0, 0), (0, 128 - 2 * NH)))

time: 422 us -> 374 us (0.89)
  Pallas kernels: 397 us -> 348 us
    pallas_call x1, Pallas kernels: 397 us -> 348 us  [fused(): pl.pallas_call(functools.partial(body, chain), out_shape=(shape((2, R, D)...]
where the time goes in v3:
time: 374 us; the launch traced here: 373 us
  Pallas kernels  348 us (93%)
  local copies, waits for them, and re-layouts  15.8 us (4%)
  other arithmetic  8.71 us (2%)
    pallas_call x1, Pallas kernels, fused(): pl.pallas_call(functools.partial(body, chain), out_shape=(shape((2, R, D)...  348 us

profile of v3, /device:TPU:0, one launch (start us, length us, event | category | flops | bytes accessed | tf_op | source)
XLA Modules:
  0.0 373.4 jit_solution(16546953520684492331)
XLA Ops:
  0.7 0.7 copy-done
  1.3 0.7 pad_maximum_fusion
  2.0 0.7 convert_element_type.20
  2.7 0.1 copy.47
  2.8 0.6 pad_convert_fusion.qkg_in
  3.5 0.7 pad_convert_fusion.1
  4.4 0.1 reduce.4
  4.5 0.1 convert_reduce_fusion
  5.0 0.6 broadcast_in_dim.34.segr_ref
  5.6 0.9 broadcast_in_dim.46.segc_ref
  6.5 1.1 dynamic-slice_bitcast_fusion
  7.6 0.7 pad.24.ct_ref
  8.4 0.7 pad.23.x_ref
  9.1 348.2 %layers.1 = (bf16[2,208,768]{2,1,0:T(8,128)(2,1)}, f32[2,208,768]{2,1,0:T(8,128)}, bf16[2304,768]{1,0:T(8,128)(2,1)}, f32[8,768]{1,0:T(8,128)}, f32[64,128]{1,0:T(8,128)}) custom-call(bf16[208,768]{1,0:T(8,128)(2,1)} %pad.23.x_ref, bf16[208,768]{1,0:T(8,128)(2,1)} %pad.24.ct_ref, s32[832,1]{1,0:T(8,128)} %broadcast_in_dim.46.segc_ref, ...), custom_call_target="tpu_custom_call" | custom-call | tf_op jit(solution)/shard_map/layers/pallas_call | solution.py:709
  357.3 1.9 slice_bitcast_fusion.1
  359.3 1.4 fusion.1
  360.7 0.8 slice_bitcast_fusion.4
  361.4 0.7 slice_bitcast_fusion.2
  362.1 1.8 copy.50
  363.9 1.4 copy.49
  365.3 1.8 bitcast_convert_fusion.2
  367.1 2.4 slice_bitcast_fusion
  369.5 1.3 slice_convert_fusion
  370.9 2.5 bitcast_convert_fusion
  (19 shorter events, 0.6 us)
Async XLA Ops:
  0.6 0.7 copy-start
  4.2 4.9 %copy-start.2 = (f32[8,768]{1,0:T(8,128)}, f32[8,768]{1,0:T(8,128)S(1)}, u32[]{:S(2)}) copy-start(f32[8,768]{1,0:T(8,128)S(1)} %scatter.14.sml_in) | copy-start | bytes 73732
  361.4 8.1 %copy-start.1 = (bf16[2304,768]{1,0:T(8,128)(2,1)S(1)}, bf16[2304,768]{1,0:T(8,128)(2,1)}, u32[]{:S(2)}) copy-start(bf16[2304,768]{1,0:T(8,128)(2,1)} %get-tuple-element.42) | copy-start | bytes 10616836

commit v4 on v3

--- a/solution.py
+++ b/solution.py
@@ -16,8 +16,12 @@
 COLS = 256
 SUB = 192
 CHUNKS = 2
-TAKEN = ((0, 0, 0, 1, 2, 3, 5, 7, 9, 10, 11, 12), (2, 3, 4, 6, 7, 9, 10, 11, 12, 12, 12, 12))
-LAYER_POINTS = 7
+TAKEN = (
+    (0, 0, 0, 0, 0, 0, 0, 0, 0, 0, 1, 1, 2, 3, 4, 5) + tuple(range(6, 13)),
+    (0, 0, 0, 0, 1, 1, 2, 3, 4, 5, 5, 6, 6, 7, 8, 9) + tuple(range(10, 13)),
+)
+LAGS = (0, 2, 3, 4, 5)
+LAYER_POINTS = 8
 
 
 def ceil_to(n, m):
@@ -318,20 +322,20 @@
         return carry
 
     steps = (step1, step2, step3, step4, step5)
-    last_point = len(TAKEN[0]) + len(steps) - 1
-
-    def progress(point, live):
+    last_point = max(len(row) for row in TAKEN) + LAGS[-1]
+
+    def progress(point):
         if not chain:
             return
 
         def taken(p):
-            if p < 0:
-                return 0
-            p = min(p, len(TAKEN[0]) - 1)
-            return jnp.where(live, jnp.where(s == 0, TAKEN[0][p], TAKEN[1][p]), 0)
-
-        for i, step in enumerate(steps):
-            lax.fori_loop(taken(point - i - 1), taken(point - i), step, 0)
+            first, second = ((0 if p < 0 else row[min(p, len(row) - 1)]) for row in TAKEN)
+            return first if first == second else jnp.where(s == 0, first, second)
+
+        for step, lag in zip(steps, LAGS):
+            lo, hi = taken(point - lag - 1), taken(point - lag)
+            if not (isinstance(lo, int) and isinstance(hi, int) and lo == hi):
+                lax.fori_loop(lo, hi, step, 0)
 
     def finish_grads():
         def one(k, carry):
@@ -562,6 +566,8 @@
                 attention_input(1, k)
 
     for l in (1, 0):
+        base = LAYER_POINTS * (1 - l)
+        progress(base)
         if l == 1:
             for k in each:
                 gather_finish(dm_all, 0, l, 2, k)
@@ -575,19 +581,17 @@
             for k in each:
                 scatter_start(lambda at, cols: mm_nt(gp_all[l, at], wu[l, cols]), l, 2, k)
         else:
-            progress(0, True)
-            gather_pass(dm_all, 0, l, 2, 0)
+            for k in each:
+                gather_pass(dm_all, 0, l, 2, k)
             for k in each:
                 gather_finish(dm_all, 0, l, 2, k)
+            down_grad(l)
+            for k in each:
                 hidden_back(l, k)
-                if k + 1 < len(CH):
-                    gather_pass(dm_all, 0, l, 2, k + 1)
                 scatter_start(lambda at, cols: mm_nt(gp_all[l, at], wu[l, cols]), l, 2, k)
-            down_grad(l)
-            progress(1, True)
+        progress(base + 1)
         up_grad(l)
-        if l == 0:
-            progress(2, True)
+        progress(base + 2)
         for k in each:
             db = scatter_finish(l, 2, k)
             xh = xh2[l, own_rows(k)]
@@ -596,8 +600,7 @@
             xres[own_rows(k)] = dh
             da_all[0, block_rows(k, pos)] = dh.astype(BF)
             gather_start(da_all, 0, l, 3, k)
-        if l == 0:
-            progress(3, True)
+        progress(base + 3)
         for k in each:
             gather_pass(da_all, 0, l, 3, k)
         for k in each:
@@ -605,17 +608,14 @@
         dot_buf[...] = mm_nt(wo[l], da_all[0]).astype(BF)
         grads[l, OUT:QKV] = mm(o_t[l], da_all[0]).astype(BF)
         send_grads(l, OUT // SUB, QKV // SUB)
-        if l == 0:
-            progress(4, True)
+        progress(base + 4)
         attention_back(l)
-        if l == 0:
-            progress(5, True)
+        progress(base + 5)
         for k in each:
             scatter_start(lambda at, cols: mm(rows_buf[0, at], wq[l, :, cols]), l, 3, k)
         grads[l, QKV:] = mm(dqkv_t[...], a_all[l]).astype(BF)
         send_grads(l, QKV // SUB, KS)
-        if l == 0:
-            progress(6, True)
+        progress(base + 6)
         for k in each:
             da = scatter_finish(l, 3, k)
             xh = xh1[l, own_rows(k)]
@@ -630,18 +630,22 @@
             else:
                 xres[own_rows(k)] = dx
 
+        progress(base + 7)
+
         @pl.when(l == s)
         def _():
             ig_out[s] = dxbuf[1].astype(F32) if l == 1 else xres[...]
 
         @pl.when(l != s)
         def _():
-            remote(dxbuf.at[1 - s], dxlo, x_s.at[1], x_r.at[1], x_id).start()
             if chain:
                 remote(gains.at[1 - s], gains_x, sm_s.at[0], sm_r.at[0], x_id).start()
                 remote(hgains.at[1 - s], hgains_x, sm_s.at[1], sm_r.at[1], x_id).start()
-
-    progress(LAYER_POINTS, True)
+            remote(dxbuf.at[1 - s], dxlo, x_s.at[1], x_r.at[1], x_id).start()
+
+    taken_all = max(len(row) for row in TAKEN)
+    for point in range(2 * LAYER_POINTS, taken_all):
+        progress(point)
     if chain:
         arrived(gains_x, sm_r.at[0])
         arrived(hgains_x, sm_r.at[1])
@@ -650,7 +654,7 @@
         for i, peer in enumerate(z_ids):
             remote(gains_z.at[b], gains_z.at[b], sm_s.at[2 + i], sm_r.at[2 + i], peer).start()
             remote(hgains_z.at[b], hgains_z.at[b], sm_s.at[5 + i], sm_r.at[5 + i], peer).start()
-        progress(LAYER_POINTS + 1, True)
+        progress(taken_all)
         for i in range(3):
             arrived(gains_x, sm_r.at[2 + i])
             arrived(hgains_x, sm_r.at[5 + i])
@@ -658,12 +662,12 @@
         gains_t[t] = gains_z[0] + gains_z[1] + gains_z[2] + gains_z[3]
         for i, peer in enumerate((core_id, y_id, diag_id)):
             remote(gains_t.at[t], gains_t.at[t], sm_s.at[8 + i], sm_r.at[8 + i], peer).start()
-        progress(LAYER_POINTS + 2, True)
+        progress(taken_all + 1)
         for i in range(3):
             arrived(gains_x, sm_r.at[8 + i])
         gg_out[...] = gains_t[0] + gains_t[1] + gains_t[2] + gains_t[3]
-        for point in range(LAYER_POINTS + 3, last_point):
-            progress(point, True)
+        for point in range(taken_all + 2, last_point):
+            progress(point)
     else:
         g_out[...] = grads[...]
         gg_out[...] = gains[...]

time: 374 us -> 335 us (0.90)
  Pallas kernels: 348 us -> 310 us
    pallas_call x1, Pallas kernels: 348 us -> 310 us  [fused(): pl.pallas_call(functools.partial(body, chain), out_shape=(shape((2, R, D)...]
where the time goes in v4:
time: 335 us
  Pallas kernels  310 us (93%)
  local copies, waits for them, and re-layouts  15.8 us (5%)
  other arithmetic  8.71 us (3%)
    pallas_call x1, Pallas kernels, fused(): pl.pallas_call(functools.partial(body, chain), out_shape=(shape((2, R, D)...  310 us

profile of v4, /device:TPU:0, one launch (start us, length us, event | category | flops | bytes accessed | tf_op | source)
XLA Modules:
  0.0 334.9 jit_solution(3561513306833321456)
XLA Ops:
  0.7 0.7 copy-done
  1.3 0.7 pad_maximum_fusion
  2.0 0.7 convert_element_type.20
  2.7 0.1 copy.47
  2.8 0.6 pad_convert_fusion.qkg_in
  3.5 0.7 pad_convert_fusion.1
  4.4 0.1 reduce.4
  4.5 0.1 convert_reduce_fusion
  5.0 0.6 broadcast_in_dim.34.segr_ref
  5.6 0.9 broadcast_in_dim.46.segc_ref
  6.5 1.1 dynamic-slice_bitcast_fusion
  7.6 0.7 pad.24.ct_ref
  8.4 0.7 pad.23.x_ref
  9.1 309.7 %layers.1 = (bf16[2,208,768]{2,1,0:T(8,128)(2,1)}, f32[2,208,768]{2,1,0:T(8,128)}, bf16[2304,768]{1,0:T(8,128)(2,1)}, f32[8,768]{1,0:T(8,128)}, f32[64,128]{1,0:T(8,128)}) custom-call(bf16[208,768]{1,0:T(8,128)(2,1)} %pad.23.x_ref, bf16[208,768]{1,0:T(8,128)(2,1)} %pad.24.ct_ref, s32[832,1]{1,0:T(8,128)} %broadcast_in_dim.46.segc_ref, ...), custom_call_target="tpu_custom_call" | custom-call | tf_op jit(solution)/shard_map/layers/pallas_call | solution.py:713
  318.8 1.9 slice_bitcast_fusion.1
  320.8 1.4 fusion.1
  322.2 0.8 slice_bitcast_fusion.4
  322.9 0.7 slice_bitcast_fusion.2
  323.6 1.8 copy.50
  325.4 1.4 copy.49
  326.8 1.8 bitcast_convert_fusion.2
  328.6 2.4 slice_bitcast_fusion
  331.0 1.3 slice_convert_fusion
  332.3 2.5 bitcast_convert_fusion
  (19 shorter events, 0.6 us)
Async XLA Ops:
  0.6 0.7 copy-start
  4.2 4.9 %copy-start.2 = (f32[8,768]{1,0:T(8,128)}, f32[8,768]{1,0:T(8,128)S(1)}, u32[]{:S(2)}) copy-start(f32[8,768]{1,0:T(8,128)S(1)} %scatter.14.sml_in) | copy-start | bytes 73732
  322.9 8.1 %copy-start.1 = (bf16[2304,768]{1,0:T(8,128)(2,1)S(1)}, bf16[2304,768]{1,0:T(8,128)(2,1)}, u32[]{:S(2)}) copy-start(bf16[2304,768]{1,0:T(8,128)(2,1)} %get-tuple-element.42) | copy-start | bytes 10616836

commit v5 on v4

--- a/solution.py
+++ b/solution.py
@@ -59,9 +59,9 @@
 
 def body(
     chain,
-    x_ref, ct_ref, segc_ref, segr_ref, sml_in, qkg_in, wq_in, wo_in, wu_in, wd_in,
+    x_ref, ct_ref, len_ref, again_ref, mgain_ref, qgain_ref, kgain_ref, wq_in, wo_in, wu_in, wd_in,
     y_out, ig_out, g_out, gg_out, gh_out,
-    wq, wo, wu, wd, sml, qkg,
+    wq, wo, wu, wd, sml, qkg, segc_ref, segr_ref, square,
     xres, xh1, r1, xh2, r2,
     a_all, b_all, dm_all, da_all,
     qkh, qkr, qkvb, lse, o_t, g_all, gp_all,
@@ -78,7 +78,8 @@
     core_id = (s, b, y * 2 + 1 - c)
     y_id = (s, b, (1 - y) * 2 + c)
     x_id = (1 - s, b, t)
-    R, D = x_ref.shape
+    own, D = x_ref.shape[1:]
+    R = ceil_to(own, 16)
     N = 4 * R
     FF = wu.shape[2]
     HD = wo.shape[1]
@@ -110,7 +111,14 @@
     def arrived(ref, sem):
         pltpu.make_async_copy(ref, ref, sem).wait()
 
-    moves = ((sml_in, sml), (qkg_in, qkg), (wq_in, wq), (wo_in, wo), (wu_in, wu), (wd_in, wd))
+    sml[s] = jnp.zeros(sml.shape[1:], F32)
+    sml[s, 0:1] = again_ref[...].astype(F32)
+    sml[s, 1:2] = mgain_ref[...].astype(F32)
+    square[...] = jnp.zeros_like(square)
+    square[0:NH, 0:HEAD] = qgain_ref[0].astype(F32)
+    square[NH : 2 * NH, 0:HEAD] = kgain_ref[0].astype(F32)
+    qkg[s] = square[...].T[0:HEAD]
+    moves = ((sml.at[s], sml), (qkg.at[s], qkg), (wq_in, wq), (wo_in, wo), (wu_in, wu), (wd_in, wd))
     pair_id = (s, b + 1 - 2 * lax.rem(b, 2), t)
     near = lax.rem(b, 2)
     blocks = []
@@ -145,14 +153,16 @@
             for j in range(len(blocks)):
                 if blocks[j][0] == i:
                     send_block(j)
-        pltpu.make_async_copy(src, dst.at[s], w_loc.at[i]).start()
+            pltpu.make_async_copy(src, dst.at[s], w_loc.at[i]).start()
 
     def weights_here(l, i):
         src, dst = moves[i]
 
-        @pl.when(l == s)
-        def _():
-            pltpu.make_async_copy(src, dst.at[s], w_loc.at[i]).wait()
+        if i > 1:
+
+            @pl.when(l == s)
+            def _():
+                pltpu.make_async_copy(src, dst.at[s], w_loc.at[i]).wait()
 
         @pl.when(l != s)
         def _():
@@ -361,6 +371,42 @@
 
     def q_rows(h):
         return pl.ds(pl.multiple_of(h * HEAD, HEAD), HEAD)
+
+    def segments():
+        wide = lax.broadcasted_iota(jnp.int32, (128, 128), 1)
+        tall = lax.broadcasted_iota(jnp.int32, (128, 128), 0)
+        slots = len_ref.shape[2]
+        square[...] = jnp.zeros_like(square)
+        square[0:1, 0:slots] = len_ref[s].astype(F32)
+        row = jnp.broadcast_to(square[0:1], (128, 128))
+        column = row.T
+        column_sums = jnp.sum(jnp.where(wide <= tall, row, 0.0), axis=1, keepdims=True)
+        row_sums = jnp.sum(jnp.where(tall <= wide, column, 0.0), axis=0, keepdims=True)
+        used = (lax.broadcasted_iota(jnp.int32, (128, 1), 0) < slots).astype(F32)
+        used_row = (lax.broadcasted_iota(jnp.int32, (1, 128), 1) < slots).astype(F32)
+        lane = lax.broadcasted_iota(jnp.int32, (1, N), 1)
+        place = lane
+        padding = jnp.zeros((1, N), F32)
+        for off, n in CH:
+            for at in range(4):
+                start = 4 * off + at * n
+                device = at % 2 * 2 + at // 2
+                here = lane >= start
+                place = jnp.where(here, lane - start + device * own + off, place)
+                padding = jnp.where(here, jnp.where(lane - start + off >= own, 1.0, 0.0), padding)
+                r = lax.broadcasted_iota(jnp.int32, (n, 1), 0) + off
+                after = jnp.where((r + device * own).astype(F32) >= row_sums, used_row, 0.0)
+                seg = jnp.sum(after, axis=1, keepdims=True)
+                segc_ref[start : start + n] = jnp.where(r >= own, -1.0, seg)
+        seg = jnp.sum(jnp.where(place.astype(F32) >= column_sums, used, 0.0), axis=0, keepdims=True)
+        segr_ref[...] = jnp.where(padding > 0, -1.0, seg)
+
+    def padded_rows(ref, k):
+        off, n = CH[k]
+        v = ref[s, off : min(off + n, own)].astype(F32)
+        if off + n > own:
+            v = jnp.concatenate([v, jnp.zeros((off + n - own, D), F32)], axis=0)
+        return v
 
     def attention_input(l, k):
         xh, r = normed(xres[own_rows(k)])
@@ -513,9 +559,10 @@
             weights_here(l, 0)
             weights_here(l, 1)
             for k in each:
-                xres[own_rows(k)] = x_ref[own_rows(k)].astype(F32)
+                xres[own_rows(k)] = padded_rows(x_ref, k)
                 attention_input(l, k)
-                dm_all[0, block_rows(k, pos)] = ct_ref[own_rows(k)]
+                dm_all[0, block_rows(k, pos)] = padded_rows(ct_ref, k).astype(BF)
+            segments()
             forward_blocks(0, 3)
         else:
             weights_here(l, 1)
@@ -537,6 +584,8 @@
         weights_here(l, 3)
         for k in each:
             scatter_start(lambda at, cols: mm(rows_buf[1, at, :HD], wo[l, :, cols]), l, 0, k)
+        if l == 0:
+            forward_blocks(6, 7)
         for k in each:
             residual = xres[own_rows(k)] + scatter_finish(l, 0, k)
             xres[own_rows(k)] = residual
@@ -546,15 +595,16 @@
             b_all[l, block_rows(k, pos)] = (xh * sml[l, 1:2]).astype(BF)
             gather_start(b_all, l, l, 1, k)
         if l == 0:
-            forward_blocks(6, len(blocks))
+            forward_blocks(7, len(blocks))
         weights_here(l, 4)
-        weights_here(l, 5)
         gather_pass(b_all, l, l, 1, 0)
         for k in each:
             gather_finish(b_all, l, l, 1, k)
             hidden(l, k)
             if k + 1 < len(CH):
                 gather_pass(b_all, l, l, 1, k + 1)
+            if k == 0:
+                weights_here(l, 5)
             scatter_start(lambda at, cols: mm(g_all[l, at], wd[l, :, cols]), l, 1, k)
         if l == 0:
             for k in each:
@@ -575,7 +625,7 @@
             down_grad(l)
             for k in each:
                 ybuf[l, own_rows(k)] = (xres[own_rows(k)] + scatter_finish(l, 1, k)).astype(BF)
-                xres[own_rows(k)] = ct_ref[own_rows(k)].astype(F32)
+                xres[own_rows(k)] = padded_rows(ct_ref, k)
             y_move = remote(ybuf.at[1 - s], ylo, x_s.at[0], x_r.at[0], x_id)
             y_move.start()
             for k in each:
@@ -634,7 +684,7 @@
 
         @pl.when(l == s)
         def _():
-            ig_out[s] = dxbuf[1].astype(F32) if l == 1 else xres[...]
+            ig_out[s] = dxbuf[1, 0:own].astype(F32) if l == 1 else xres[0:own]
 
         @pl.when(l != s)
         def _():
@@ -673,12 +723,12 @@
         gg_out[...] = gains[...]
         gh_out[...] = hgains[...]
     y_move.wait()
-    y_out[s] = ybuf[s]
-    y_out[1 - s] = ylo[...]
+    y_out[s] = ybuf[s, 0:own]
+    y_out[1 - s] = ylo[0:own]
     finish_weights()
     arrived(dxlo, x_s.at[1])
     arrived(dxlo, x_r.at[1])
-    ig_out[1 - s] = dxlo[...].astype(F32)
+    ig_out[1 - s] = dxlo[0:own].astype(F32)
     if chain:
         finish_grads()
         for i in range(2, 5):
@@ -689,8 +739,9 @@
         arrived(hgains_x, sm_s.at[1])
 
 
-def fused(chain, x, ct, segc, segr, small, qk_gain, wq, wo, wu, wd):
-    R, D = x.shape
+def fused(chain, x, ct, lengths, again, mgain, qgain, kgain, wq, wo, wu, wd):
+    own, D = x.shape[1:]
+    R = ceil_to(own, 16)
     N = 4 * R
     QD, HD, FF = wq.shape[0], wo.shape[0], wu.shape[1]
     NH = HD // HEAD
@@ -713,17 +764,17 @@
     return pl.pallas_call(
         functools.partial(body, chain),
         out_shape=(
-            shape((2, R, D), BF),
-            shape((2, R, D), F32),
+            shape((2, own, D), BF),
+            shape((2, own, D), F32),
             shape(ahead + (G, D), BF),
             shape(ahead + (8, D), F32),
             shape(ahead + (HEAD, 128), F32),
         ),
-        in_specs=[vmem] * 4 + [hbm] * 6,
+        in_specs=[vmem] * 7 + [hbm] * 4,
         out_specs=(vmem, vmem, hbm if chain else vmem, vmem, vmem),
         scratch_shapes=[
             V((2, QD, D), BF), V((2, HD, D), BF), V((2, D, FF), BF), V((2, FF, D), BF),
-            V((2, 8, D), F32), V((2, HEAD, 128), F32),
+            V((2, 8, D), F32), V((2, HEAD, 128), F32), V((N, 1), F32), V((1, N), F32), V((128, 128), F32),
             V((R, D), F32), V((2, R, D), F32), V((2, R, 1), F32), V((2, R, D), F32), V((2, R, 1), F32),
             V((2, N, D), BF), V((2, N, D), BF), V((1, N, D), BF), V((1, N, D), BF),
             V((2, 2 * HD, N), F32), V((2, 2, 8, N), F32), V((2, QD, N), BF), V((2, 8, N), F32),
@@ -740,7 +791,76 @@
         compiler_params=pltpu.CompilerParams(
             collective_id=0, has_side_effects=True, vmem_limit_bytes=63 * 2**20
         ),
-    )(x, ct, segc, segr, small, qk_gain, wq, wo, wu, wd)
+    )(x, ct, lengths, again, mgain, qgain, kgain, wq, wo, wu, wd)
+
+
+def widen(
+    y_in, ig_in, g_in, gg_ref, gh_ref,
+    y_out, ig_out, gd_out, gu_out, go_out, gq_out, gattn_out, gmlp_out, gqg_out, gkg_out,
+    low, wide, y_buf, ig_buf, in_sem, out_sem, move_sem,
+):
+    fetch = [
+        pltpu.make_async_copy(y_in, y_buf, move_sem.at[0]),
+        pltpu.make_async_copy(ig_in, ig_buf, move_sem.at[1]),
+    ]
+    put = [
+        pltpu.make_async_copy(y_buf, y_out, move_sem.at[2]),
+        pltpu.make_async_copy(ig_buf, ig_out, move_sem.at[3]),
+    ]
+    pieces = []
+    at = 0
+    for out in (gd_out, gu_out, go_out, gq_out):
+        for row in range(0, out.shape[0], SUB):
+            pieces.append((at, row, out))
+            at += SUB
+    loads = [pltpu.make_async_copy(g_in.at[a : a + SUB], low.at[a : a + SUB], in_sem.at[i]) for i, (a, _, _) in enumerate(pieces)]
+    stores = [
+        pltpu.make_async_copy(wide.at[a : a + SUB], out.at[row : row + SUB], out_sem.at[i])
+        for i, (a, row, out) in enumerate(pieces)
+    ]
+    for copy in fetch + loads:
+        copy.start()
+    gattn_out[...] = gg_ref[0:1]
+    gmlp_out[...] = gg_ref[1:2]
+    heads = gqg_out.shape[0]
+    by_head = gh_ref[...].T
+    for h in range(heads):
+        gqg_out[h] = by_head[h : h + 1]
+        gkg_out[h] = by_head[heads + h : heads + h + 1]
+    for i in range(2):
+        fetch[i].wait()
+        put[i].start()
+    for i, (a, _, _) in enumerate(pieces):
+        loads[i].wait()
+        wide[a : a + SUB] = low[a : a + SUB].astype(F32)
+        stores[i].start()
+    for copy in stores + put:
+        copy.wait()
+
+
+def final(y, ig, g, gg, gh, FF, D, HD):
+    G = g.shape[0]
+    NH = HD // HEAD
+    vmem = pl.BlockSpec(memory_space=pltpu.VMEM)
+    hbm = pl.BlockSpec(memory_space=pl.ANY)
+    shape = jax.ShapeDtypeStruct
+    dma = pltpu.SemaphoreType.DMA
+    return pl.pallas_call(
+        widen,
+        out_shape=(
+            shape(y.shape, BF), shape(ig.shape, F32), shape((FF, D), F32), shape((D, FF), F32), shape((HD, D), F32),
+            shape((3 * HD, D), F32), shape((1, D), F32), shape((1, D), F32), shape((NH, 1, HEAD), F32),
+            shape((NH, 1, HEAD), F32),
+        ),
+        in_specs=[hbm] * 3 + [vmem] * 2,
+        out_specs=(hbm,) * 6 + (vmem,) * 4,
+        scratch_shapes=[
+            pltpu.VMEM((G, D), BF), pltpu.VMEM((G, D), F32), pltpu.VMEM(y.shape, BF),
+            pltpu.VMEM(ig.shape, F32), dma((G // SUB,)), dma((G // SUB,)), dma((4,)),
+        ],
+        name="widen",
+        compiler_params=pltpu.CompilerParams(vmem_limit_bytes=60 * 2**20),
+    )(y, ig, g, gg, gh)
 
 
 def shards(
@@ -748,50 +868,32 @@
     mlp_gain, up_weight, down_weight,
 ):
     s = lax.axis_index("section")
-    _, own, D = patches.shape
-    seq_len = 4 * own
-    R = ceil_to(own, 16)
-    N = 4 * R
+    own, D = patches.shape[1:]
     HD = out_weight.shape[1]
     NH = HD // HEAD
-    pad = ((0, R - own), (0, 0))
-    x = jnp.pad(lax.dynamic_index_in_dim(patches, s, 0, keepdims=False), pad)
-    ct = jnp.pad(lax.dynamic_index_in_dim(cotangent, s, 0, keepdims=False), pad)
-    lengths = lax.dynamic_index_in_dim(image_lengths, s, 0, keepdims=False)[0]
-    bounds = jnp.cumsum(lengths, dtype=jnp.int32)
-    places = jnp.arange(seq_len, dtype=jnp.int32)
-    seg = jnp.sum((places[:, None] >= bounds[None, :]).astype(jnp.int32), axis=-1)
-    seg = seg.reshape(2, 2, own).transpose(1, 0, 2).reshape(4, own)
-    seg = jnp.pad(seg, ((0, 0), (0, R - own)), constant_values=-1)
-    seg = jnp.concatenate([seg[:, a : a + n].reshape(4 * n) for a, n in chunks_of(R)])
-    small = jnp.zeros((8, D), F32).at[0].set(attn_gain[0].astype(F32)).at[1].set(mlp_gain[0].astype(F32))
-    qk_gain = jnp.concatenate([query_gain[0], key_gain[0]], axis=0).astype(F32).T
-    qk_gain = jnp.pad(qk_gain, ((0, 0), (0, 128 - 2 * NH)))
     wq = qkv_weight[0].reshape(D, 3 * HD).T
     chain = lax.axis_size("batch") == 4
     y, ig, g, gg, gh = fused(
-        chain, x, ct, seg[:, None], seg[None, :], small, qk_gain, wq, out_weight[0], up_weight[0],
-        down_weight[0],
+        chain, patches, cotangent, image_lengths, attn_gain, mlp_gain, query_gain, key_gain, wq,
+        out_weight[0], up_weight[0], down_weight[0],
     )
     if not chain:
         theirs = lax.ppermute(g[1 - s], "section", [(0, 1), (1, 0)])
         g = lax.psum((g[s].astype(F32) + theirs.astype(F32)).astype(BF), "batch")
         gg = lax.psum(gg, ("section", "batch", "tensor"))[s]
         gh = lax.psum(gh, ("section", "batch"))[s]
-    FF = up_weight.shape[2]
-    gd, gu, go, gq = (g[:FF], g[FF : FF + D], g[FF + D : FF + D + HD], g[FF + D + HD :])
-    gh = gh[:, : 2 * NH].T.reshape(2, NH, HEAD)
+    y, ig, gd, gu, go, gq, gattn, gmlp, gqg, gkg = final(y, ig, g, gg, gh, up_weight.shape[2], D, HD)
     return (
-        y[:, :own][None],
-        ig[:, :own][None],
-        gg[0][None],
-        gq.astype(F32).T.reshape(D, 3, HD)[None],
-        gh[0][None],
-        gh[1][None],
-        go.astype(F32)[None],
-        gg[1][None],
-        gu.astype(F32)[None],
-        gd.astype(F32)[None],
+        y[None],
+        ig[None],
+        gattn,
+        gq.T.reshape(D, 3, HD)[None],
+        gqg.reshape(1, NH, HEAD),
+        gkg.reshape(1, NH, HEAD),
+        go[None],
+        gmlp,
+        gu[None],
+        gd[None],
     )
 
 

time: 335 us -> 315 us (0.940)
  local copies, waits for them, and re-layouts: 15.8 us -> 0 us
  other arithmetic: 8.71 us -> 0 us
  Pallas kernels: 310 us -> 314 us
    broadcast_in_dim x4 -> x0, local copies, waits for them, and re-layouts: 5.86 us -> none  [the longest x1 2.4 us: shards(): ig[:, :own][None]]
    broadcast_in_dim x2 -> x0, other arithmetic: 4.36 us -> none  [the longest x1 2.54 us: shards(): gd.astype(F32)[None]]
    unnamed x9 -> x0, local copies, waits for them, and re-layouts: 3.85 us -> none
    pallas_call x1 -> x2, Pallas kernels: 310 us -> 314 us  [the longest x1 306 us: fused(): pl.pallas_call(functools.partial(body, chain), out_shape=(shape((2, own,...]
where the time goes in v5:
time: 315 us; the launch traced here: 314 us
  Pallas kernels  314 us (100%)
    pallas_call x1, Pallas kernels, fused(): pl.pallas_call(functools.partial(body, chain), out_shape=(shape((2, own,...  306 us
    pallas_call x1, Pallas kernels, final(): pl.pallas_call(widen, out_shape=(shape(y.shape, BF), shape(ig.shape, F32)...  7.31 us

profile of v5, /device:TPU:0, one launch (start us, length us, event | category | flops | bytes accessed | tf_op | source)
XLA Modules:
  0.0 314.3 jit_solution(5237532217640903507)
XLA Ops:
  0.6 306.2 %layers.1 = (bf16[2,200,768]{2,1,0:T(8,128)(2,1)}, f32[2,200,768]{2,1,0:T(8,128)}, bf16[2304,768]{1,0:T(8,128)(2,1)}, f32[8,768]{1,0:T(8,128)}, f32[64,128]{1,0:T(8,128)}) custom-call(bf16[2,200,768]{2,1,0:T(8,128)(2,1)} %x_ref.1, bf16[2,200,768]{2,1,0:T(8,128)(2,1)} %ct_ref.1, s32[2,1,60]{2,1,0:T(1,128)} %len_ref.1, bf16[1,768]{1,0:T(2,128)(2,1)} %again_ref.1, ...), custom_call_target="tpu_custom_call" | custom-call | tf_op jit(solution)/shard_map/layers/pallas_call | solution.py:764
  306.8 7.3 %widen.1 = (bf16[2,200,768]{2,1,0:T(8,128)(2,1)}, f32[2,200,768]{2,1,0:T(8,128)}, f32[768,768]{1,0:T(8,128)}, f32[768,768]{1,0:T(8,128)}, f32[192,768]{1,0:T(8,1...) custom-call(bf16[2,200,768]{2,1,0:T(8,128)(2,1)} %get-tuple-element., ...), custom_call_target="tpu_custom_call" | custom-call | tf_op jit(solution)/shard_map/widen/pallas_call | solution.py:848

commit v6 on v5

--- a/solution.py
+++ b/solution.py
@@ -12,8 +12,8 @@
 MESH = pl.DeviceIdType.MESH
 BF = jnp.bfloat16
 F32 = jnp.float32
-KEY_BLOCK = 64
-COLS = 256
+KEY_BLOCK = 208
+COLS = 384
 SUB = 192
 CHUNKS = 2
 TAKEN = (
@@ -65,12 +65,12 @@
     xres, xh1, r1, xh2, r2,
     a_all, b_all, dm_all, da_all,
     qkh, qkr, qkvb, lse, o_t, g_all, gp_all,
-    rows_buf, part, sendbuf, ysend, crecv, yrecv,
+    rows_buf, rows_two, part, sendbuf, ysend, crecv, yrecv,
     e_buf, d_buf, dot_buf, dqkv_t,
     ybuf, dxbuf, ylo, dxlo,
     grads, gains, hgains,
     w_loc, w_send, w_recv, wz_s, wz_r, ag_s, ag_r, rs_s, rs_r, x_s, x_r,
-    gx, gz, gpart, gfin, gains_x, hgains_x, gains_z, hgains_z, gains_t,
+    gx, gz, gpart, gains_x, hgains_x, gains_z, hgains_z, gains_t,
     gx_s, gx_r, gz_s, gz_r, g_loc, sm_s, sm_r,
 ):
     s, b, t = lax.axis_index("section"), lax.axis_index("batch"), lax.axis_index("tensor")
@@ -305,7 +305,7 @@
             arrived(gpart.at[k], gz_r.at[1, k])
             grads[s, rows] = (grads[s, rows].astype(F32) + gpart[k].astype(F32)).astype(BF)
             done = grads.at[s, rows]
-            remote(done, gfin.at[k], gz_s.at[1, k], gz_r.at[2, k], partner_id).start()
+            remote(done, gz.at[rows], gz_s.at[1, k], gz_r.at[2, k], partner_id).start()
             remote(done, gz.at[rows], gz_s.at[2, k], gz_r.at[0, k], outer_id).start()
             pltpu.make_async_copy(done, g_out.at[rows], g_loc.at[0, k]).start()
 
@@ -315,9 +315,10 @@
         @pl.when(middle)
         def _():
             rows = half_rows(k, other_at)
-            arrived(gfin.at[k], gz_r.at[2, k])
-            remote(gfin.at[k], gz.at[rows], gz_s.at[3, k], gz_r.at[1, k], outer_id).start()
-            pltpu.make_async_copy(gfin.at[k], g_out.at[rows], g_loc.at[1, k]).start()
+            done = gz.at[rows]
+            arrived(done, gz_r.at[2, k])
+            remote(done, done, gz_s.at[3, k], gz_r.at[1, k], outer_id).start()
+            pltpu.make_async_copy(done, g_out.at[rows], g_loc.at[1, k]).start()
 
         return carry
 
@@ -442,22 +443,22 @@
         def head(h, carry):
             q_t = qkvb[l, q_rows(h)]
             v_t = qkvb[l, q_rows(2 * NH + h)]
-            rows_buf[0, :, :HEAD] = qkvb[l, q_rows(NH + h)].astype(F32).T.astype(BF)
+            rows_buf[:, :HEAD] = qkvb[l, q_rows(NH + h)].astype(F32).T.astype(BF)
 
             def block(i, total):
                 at = pl.ds(pl.multiple_of(i * KEY_BLOCK, KEY_BLOCK), KEY_BLOCK)
-                sc = mm(rows_buf[0, at, :HEAD], q_t)
+                sc = mm(rows_buf[at, :HEAD], q_t)
                 e = jnp.where(segc_ref[at] == segr_ref[...], jnp.exp(sc), 0.0)
                 e_buf[at] = e.astype(BF)
                 return total + jnp.sum(e, axis=0, keepdims=True)
 
-            total = lax.fori_loop(0, NB, block, jnp.zeros((1, N), F32))
+            total = lax.fori_loop(0, NB, block, jnp.zeros((1, N), F32), unroll=True)
             lse[l, pl.ds(h, 1)] = jnp.log(total)
             o_t[l, q_rows(h)] = (mm(v_t, e_buf[...]) * (1.0 / total)).astype(BF)
             return carry
 
         lax.fori_loop(0, NH, head, 0)
-        rows_buf[1, :, :HD] = o_t[l].astype(F32).T.astype(BF)
+        rows_two[:, :HD] = o_t[l].astype(F32).T.astype(BF)
 
     def hidden(l, k):
         off, n = CH[k]
@@ -517,22 +518,22 @@
             q_t = qkvb[l, q_rows(h)]
             k_t = qkvb[l, q_rows(NH + h)]
             v_t = qkvb[l, q_rows(2 * NH + h)]
-            rows_buf[0, :, :HEAD] = k_t.astype(F32).T.astype(BF)
-            rows_buf[1, :, :HEAD] = v_t.astype(F32).T.astype(BF)
+            rows_buf[:, :HEAD] = k_t.astype(F32).T.astype(BF)
+            rows_two[:, :HEAD] = v_t.astype(F32).T.astype(BF)
             do_t = dot_buf[q_rows(h)]
             delta = jnp.sum(do_t.astype(F32) * o_t[l, q_rows(h)].astype(F32), axis=0, keepdims=True)
             log_total = lse[l, pl.ds(h, 1)]
 
             def block(i, carry):
                 at = pl.ds(pl.multiple_of(i * KEY_BLOCK, KEY_BLOCK), KEY_BLOCK)
-                sc = mm(rows_buf[0, at, :HEAD], q_t)
+                sc = mm(rows_buf[at, :HEAD], q_t)
                 p = jnp.where(segc_ref[at] == segr_ref[...], jnp.exp(sc - log_total), 0.0)
-                dp = mm(rows_buf[1, at, :HEAD], do_t)
+                dp = mm(rows_two[at, :HEAD], do_t)
                 e_buf[at] = p.astype(BF)
                 d_buf[at] = (p * (dp - delta)).astype(BF)
                 return carry
 
-            lax.fori_loop(0, NB, block, 0)
+            lax.fori_loop(0, NB, block, 0, unroll=True)
             dqkv_t[q_rows(2 * NH + h)] = mm_nt(do_t, e_buf[...]).astype(BF)
             dk = mm_nt(q_t, d_buf[...])
             dq = mm(k_t, d_buf[...]) * (HEAD**-0.5)
@@ -549,7 +550,7 @@
 
         hgains[l] = jnp.zeros((HEAD, 128), F32)
         lax.fori_loop(0, NH, head, 0)
-        rows_buf[0] = dqkv_t[...].astype(F32).T.astype(BF)
+        rows_buf[...] = dqkv_t[...].astype(F32).T.astype(BF)
 
     each = range(len(CH))
     gains[...] = jnp.zeros_like(gains)
@@ -583,7 +584,7 @@
                 gather_pass(dm_all, 0, 1, 2, k)
         weights_here(l, 3)
         for k in each:
-            scatter_start(lambda at, cols: mm(rows_buf[1, at, :HD], wo[l, :, cols]), l, 0, k)
+            scatter_start(lambda at, cols: mm(rows_two[at, :HD], wo[l, :, cols]), l, 0, k)
         if l == 0:
             forward_blocks(6, 7)
         for k in each:
@@ -656,13 +657,13 @@
         for k in each:
             gather_finish(da_all, 0, l, 3, k)
         dot_buf[...] = mm_nt(wo[l], da_all[0]).astype(BF)
-        grads[l, OUT:QKV] = mm(o_t[l], da_all[0]).astype(BF)
-        send_grads(l, OUT // SUB, QKV // SUB)
         progress(base + 4)
         attention_back(l)
         progress(base + 5)
         for k in each:
-            scatter_start(lambda at, cols: mm(rows_buf[0, at], wq[l, :, cols]), l, 3, k)
+            scatter_start(lambda at, cols: mm(rows_buf[at], wq[l, :, cols]), l, 3, k)
+        grads[l, OUT:QKV] = mm(o_t[l], da_all[0]).astype(BF)
+        send_grads(l, OUT // SUB, QKV // SUB)
         grads[l, QKV:] = mm(dqkv_t[...], a_all[l]).astype(BF)
         send_grads(l, QKV // SUB, KS)
         progress(base + 6)
@@ -705,6 +706,7 @@
             remote(gains_z.at[b], gains_z.at[b], sm_s.at[2 + i], sm_r.at[2 + i], peer).start()
             remote(hgains_z.at[b], hgains_z.at[b], sm_s.at[5 + i], sm_r.at[5 + i], peer).start()
         progress(taken_all)
+        progress(taken_all + 1)
         for i in range(3):
             arrived(gains_x, sm_r.at[2 + i])
             arrived(hgains_x, sm_r.at[5 + i])
@@ -712,12 +714,11 @@
         gains_t[t] = gains_z[0] + gains_z[1] + gains_z[2] + gains_z[3]
         for i, peer in enumerate((core_id, y_id, diag_id)):
             remote(gains_t.at[t], gains_t.at[t], sm_s.at[8 + i], sm_r.at[8 + i], peer).start()
-        progress(taken_all + 1)
+        for point in range(taken_all + 2, last_point):
+            progress(point)
         for i in range(3):
             arrived(gains_x, sm_r.at[8 + i])
         gg_out[...] = gains_t[0] + gains_t[1] + gains_t[2] + gains_t[3]
-        for point in range(taken_all + 2, last_point):
-            progress(point)
     else:
         g_out[...] = grads[...]
         gg_out[...] = gains[...]
@@ -755,12 +756,12 @@
     KS = G // SUB
     ahead = () if chain else (2,)
     extra = [
-        V((G, D), BF), V((G, D), BF), V((KS, SUB // 2, D), BF), V((KS, SUB // 2, D), BF),
+        V((G, D), BF), V((G, D), BF), V((KS, SUB // 2, D), BF),
         V((8, D), F32), V((HEAD, 128), F32), V((4, 8, D), F32), V((4, HEAD, 128), F32), V((4, 8, D), F32),
         dma((KS,)), dma((KS,)), dma((4, KS)), dma((3, KS)), dma((2, KS)), dma((11,)), dma((11,)),
     ]
     if not chain:
-        extra = [V((8, 128), F32)] * 9 + [dma((1,))] * 7
+        extra = [V((8, 128), F32)] * 8 + [dma((1,))] * 7
     return pl.pallas_call(
         functools.partial(body, chain),
         out_shape=(
@@ -779,7 +780,7 @@
             V((2, N, D), BF), V((2, N, D), BF), V((1, N, D), BF), V((1, N, D), BF),
             V((2, 2 * HD, N), F32), V((2, 2, 8, N), F32), V((2, QD, N), BF), V((2, 8, N), F32),
             V((2, HD, N), BF), V((2, N, FF), BF), V((2, N, FF), BF),
-            V((2, N, QD), BF), V((2 * R, D), F32), V((2 * R, D), BF), V((R, D), BF),
+            V((N, QD), BF), V((N, HD), BF), V((2 * R, D), F32), V((2 * R, D), BF), V((R, D), BF),
             V((2, 2 * R, D), BF), V((2, R, D), BF),
             V((N, N), BF), V((N, N), BF), V((HD, N), BF), V((QD, N), BF),
             V((2, R, D), BF), V((2, R, D), BF), V((R, D), BF), V((R, D), BF),

time: 315 us -> 290 us (0.921)
  Pallas kernels: 314 us -> 289 us
    pallas_call x1, Pallas kernels: 306 us -> 281 us  [fused(): pl.pallas_call(functools.partial(body, chain), out_shape=(shape((2, own,...]
where the time goes in v6:
time: 290 us; the launch traced here: 289 us
  Pallas kernels  289 us (100%)
    pallas_call x1, Pallas kernels, fused(): pl.pallas_call(functools.partial(body, chain), out_shape=(shape((2, own,...  281 us
    pallas_call x1, Pallas kernels, final(): pl.pallas_call(widen, out_shape=(shape(y.shape, BF), shape(ig.shape, F32)...  7.31 us

profile of v6, /device:TPU:0, one launch (start us, length us, event | category | flops | bytes accessed | tf_op | source)
XLA Modules:
  0.0 289.4 jit_solution(14211085590090956300)
XLA Ops:
  0.6 281.3 %layers.1 = (bf16[2,200,768]{2,1,0:T(8,128)(2,1)}, f32[2,200,768]{2,1,0:T(8,128)}, bf16[2304,768]{1,0:T(8,128)(2,1)}, f32[8,768]{1,0:T(8,128)}, f32[64,128]{1,0:T(8,128)}) custom-call(bf16[2,200,768]{2,1,0:T(8,128)(2,1)} %x_ref.1, bf16[2,200,768]{2,1,0:T(8,128)(2,1)} %ct_ref.1, s32[2,1,60]{2,1,0:T(1,128)} %len_ref.1, bf16[1,768]{1,0:T(2,128)(2,1)} %again_ref.1, ...), custom_call_target="tpu_custom_call" | custom-call | tf_op jit(solution)/shard_map/layers/pallas_call | solution.py:765
  281.9 7.3 %widen.1 = (bf16[2,200,768]{2,1,0:T(8,128)(2,1)}, f32[2,200,768]{2,1,0:T(8,128)}, f32[768,768]{1,0:T(8,128)}, f32[768,768]{1,0:T(8,128)}, f32[192,768]{1,0:T(8,1...) custom-call(bf16[2,200,768]{2,1,0:T(8,128)(2,1)} %get-tuple-element., ...), custom_call_target="tpu_custom_call" | custom-call | tf_op jit(solution)/shard_map/widen/pallas_call | solution.py:849

commit v7 on v6

--- a/solution.py
+++ b/solution.py
@@ -17,7 +17,7 @@
 SUB = 192
 CHUNKS = 2
 TAKEN = (
-    (0, 0, 0, 0, 0, 0, 0, 0, 0, 0, 1, 1, 2, 3, 4, 5) + tuple(range(6, 13)),
+    (0, 0, 0, 0, 0, 0, 0, 0, 0, 1, 1, 2, 3, 4, 5, 6) + tuple(range(7, 13)),
     (0, 0, 0, 0, 1, 1, 2, 3, 4, 5, 5, 6, 6, 7, 8, 9) + tuple(range(10, 13)),
 )
 LAGS = (0, 2, 3, 4, 5)
@@ -492,20 +492,20 @@
             cols = pl.ds(pl.multiple_of(i * COLS, COLS), COLS)
             at = pl.ds(pl.multiple_of(FD + i * COLS, COLS), COLS)
             grads[l, at] = mm_tn(g_all[l, :, cols], dm_all[0]).astype(BF)
+            send_grads(l, i * (COLS // SUB), (i + 1) * (COLS // SUB))
             return carry
 
         lax.fori_loop(0, FF // COLS, tile, 0)
-        send_grads(l, 0, UP // SUB)
 
     def up_grad(l):
         def tile(i, carry):
             cols = pl.ds(pl.multiple_of(i * COLS, COLS), COLS)
             at = pl.ds(pl.multiple_of(UP + i * COLS, COLS), COLS)
             grads[l, at] = mm_tn(b_all[l, :, cols], gp_all[l]).astype(BF)
+            send_grads(l, UP // SUB + i * (COLS // SUB), UP // SUB + (i + 1) * (COLS // SUB))
             return carry
 
         lax.fori_loop(0, D // COLS, tile, 0)
-        send_grads(l, UP // SUB, OUT // SUB)
 
     def gains_of(l, i, h):
         out = qkg[l, :, i * NH : i * NH + 1]
@@ -694,6 +694,16 @@
                 remote(hgains.at[1 - s], hgains_x, sm_s.at[1], sm_r.at[1], x_id).start()
             remote(dxbuf.at[1 - s], dxlo, x_s.at[1], x_r.at[1], x_id).start()
 
+    y_move.wait()
+    y_out[s] = ybuf[s, 0:own]
+    y_out[1 - s] = ylo[0:own]
+    finish_weights()
+
+    def finish_inputs():
+        arrived(dxlo, x_s.at[1])
+        arrived(dxlo, x_r.at[1])
+        ig_out[1 - s] = dxlo[0:own].astype(F32)
+
     taken_all = max(len(row) for row in TAKEN)
     for point in range(2 * LAYER_POINTS, taken_all):
         progress(point)
@@ -715,6 +725,8 @@
         for i, peer in enumerate((core_id, y_id, diag_id)):
             remote(gains_t.at[t], gains_t.at[t], sm_s.at[8 + i], sm_r.at[8 + i], peer).start()
         for point in range(taken_all + 2, last_point):
+            if point == last_point - 2:
+                finish_inputs()
             progress(point)
         for i in range(3):
             arrived(gains_x, sm_r.at[8 + i])
@@ -723,13 +735,8 @@
         g_out[...] = grads[...]
         gg_out[...] = gains[...]
         gh_out[...] = hgains[...]
-    y_move.wait()
-    y_out[s] = ybuf[s, 0:own]
-    y_out[1 - s] = ylo[0:own]
-    finish_weights()
-    arrived(dxlo, x_s.at[1])
-    arrived(dxlo, x_r.at[1])
-    ig_out[1 - s] = dxlo[0:own].astype(F32)
+    if not chain:
+        finish_inputs()
     if chain:
         finish_grads()
         for i in range(2, 5):

time: 290 us -> 286 us (0.986)
  Pallas kernels: 289 us -> 285 us
    pallas_call x1, Pallas kernels: 281 us -> 277 us  [fused(): pl.pallas_call(functools.partial(body, chain), out_shape=(shape((2, own,...]
where the time goes in v7:
time: 286 us
  Pallas kernels  285 us (100%)
    pallas_call x1, Pallas kernels, fused(): pl.pallas_call(functools.partial(body, chain), out_shape=(shape((2, own,...  277 us
    pallas_call x1, Pallas kernels, final(): pl.pallas_call(widen, out_shape=(shape(y.shape, BF), shape(ig.shape, F32)...  7.31 us

profile of v7, /device:TPU:0, one launch (start us, length us, event | category | flops | bytes accessed | tf_op | source)
XLA Modules:
  0.0 285.6 jit_solution(12746387522225561786)
XLA Ops:
  0.6 277.5 %layers.1 = (bf16[2,200,768]{2,1,0:T(8,128)(2,1)}, f32[2,200,768]{2,1,0:T(8,128)}, bf16[2304,768]{1,0:T(8,128)(2,1)}, f32[8,768]{1,0:T(8,128)}, f32[64,128]{1,0:T(8,128)}) custom-call(bf16[2,200,768]{2,1,0:T(8,128)(2,1)} %x_ref.1, bf16[2,200,768]{2,1,0:T(8,128)(2,1)} %ct_ref.1, s32[2,1,60]{2,1,0:T(1,128)} %len_ref.1, bf16[1,768]{1,0:T(2,128)(2,1)} %again_ref.1, ...), custom_call_target="tpu_custom_call" | custom-call | tf_op jit(solution)/shard_map/layers/pallas_call | solution.py:772
  278.1 7.3 %widen.1 = (bf16[2,200,768]{2,1,0:T(8,128)(2,1)}, f32[2,200,768]{2,1,0:T(8,128)}, f32[768,768]{1,0:T(8,128)}, f32[768,768]{1,0:T(8,128)}, f32[192,768]{1,0:T(8,1...) custom-call(bf16[2,200,768]{2,1,0:T(8,128)(2,1)} %get-tuple-element., ...), custom_call_target="tpu_custom_call" | custom-call | tf_op jit(solution)/shard_map/widen/pallas_call | solution.py:856

commit v8 on v7

--- a/solution.py
+++ b/solution.py
@@ -646,11 +646,11 @@
         for k in each:
             db = scatter_finish(l, 2, k)
             xh = xh2[l, own_rows(k)]
-            gains[l, 1:2] = gains[l, 1:2] + jnp.sum(db * xh, axis=0, keepdims=True)
             dh = xres[own_rows(k)] + normed_back(db, sml[l, 1:2], xh, r2[l, own_rows(k)])
             xres[own_rows(k)] = dh
             da_all[0, block_rows(k, pos)] = dh.astype(BF)
             gather_start(da_all, 0, l, 3, k)
+            gains[l, 1:2] = gains[l, 1:2] + jnp.sum(db * xh, axis=0, keepdims=True)
         progress(base + 3)
         for k in each:
             gather_pass(da_all, 0, l, 3, k)
@@ -670,7 +670,6 @@
         for k in each:
             da = scatter_finish(l, 3, k)
             xh = xh1[l, own_rows(k)]
-            gains[l, 0:1] = gains[l, 0:1] + jnp.sum(da * xh, axis=0, keepdims=True)
             dx = xres[own_rows(k)] + normed_back(da, sml[l, 0:1], xh, r1[l, own_rows(k)])
             rounded = dx.astype(BF)
             dxbuf[l, own_rows(k)] = rounded
@@ -680,6 +679,7 @@
                 gather_start(dm_all, 0, 0, 2, k)
             else:
                 xres[own_rows(k)] = dx
+            gains[l, 0:1] = gains[l, 0:1] + jnp.sum(da * xh, axis=0, keepdims=True)
 
         progress(base + 7)
 

time: 286 us -> 286 us (level)
  no operation moved by 1% of the time
where the time goes in v8:
time: 286 us
  Pallas kernels  285 us (100%)
    pallas_call x1, Pallas kernels, fused(): pl.pallas_call(functools.partial(body, chain), out_shape=(shape((2, own,...  278 us
    pallas_call x1, Pallas kernels, final(): pl.pallas_call(widen, out_shape=(shape(y.shape, BF), shape(ig.shape, F32)...  7.31 us

profile of v8, /device:TPU:0, one launch (start us, length us, event | category | flops | bytes accessed | tf_op | source)
XLA Modules:
  0.0 285.7 jit_solution(2353315893376776285)
XLA Ops:
  0.6 277.6 %layers.1 = (bf16[2,200,768]{2,1,0:T(8,128)(2,1)}, f32[2,200,768]{2,1,0:T(8,128)}, bf16[2304,768]{1,0:T(8,128)(2,1)}, f32[8,768]{1,0:T(8,128)}, f32[64,128]{1,0:T(8,128)}) custom-call(bf16[2,200,768]{2,1,0:T(8,128)(2,1)} %x_ref.1, bf16[2,200,768]{2,1,0:T(8,128)(2,1)} %ct_ref.1, s32[2,1,60]{2,1,0:T(1,128)} %len_ref.1, bf16[1,768]{1,0:T(2,128)(2,1)} %again_ref.1, ...), custom_call_target="tpu_custom_call" | custom-call | tf_op jit(solution)/shard_map/layers/pallas_call | solution.py:772
  278.2 7.3 %widen.1 = (bf16[2,200,768]{2,1,0:T(8,128)(2,1)}, f32[2,200,768]{2,1,0:T(8,128)}, f32[768,768]{1,0:T(8,128)}, f32[768,768]{1,0:T(8,128)}, f32[192,768]{1,0:T(8,1...) custom-call(bf16[2,200,768]{2,1,0:T(8,128)(2,1)} %get-tuple-element., ...), custom_call_target="tpu_custom_call" | custom-call | tf_op jit(solution)/shard_map/widen/pallas_call | solution.py:856
